TPU v7x, 32 devices: a whole 2x2x4 slice. The times are simulated.
32 devices in a mesh: dp: 2 (over y), ctx: 8 (over z, core), fsdp: 2 (over x).
Axes of the slice: x: 2, y: 2, z: 4, core: 2. Of those that a mesh axis runs over, the one named last changes fastest.
Arguments:
- inputs: bfloat16 [8, 2048, 768], P(('dp', 'fsdp'), 'ctx'), may hold values from -6 to 6
- w_qkv: bfloat16 [768, 2304], P('fsdp'), may hold values from -0.21875 to 0.21875
- w_out: bfloat16 [768, 768], P('fsdp'), may hold values from -1.75 to 1.75
- w_up: bfloat16 [768, 3072], P('fsdp'), may hold values from -0.21875 to 0.21875
- w_down: bfloat16 [3072, 768], P('fsdp'), may hold values from -0.109375 to 0.109375
- ln1_gain: bfloat16 [768], P('fsdp'), may hold values from 0.5 to 1.5
- ln1_bias: bfloat16 [768], P('fsdp'), may hold values from -3 to 3
- q_bias: bfloat16 [768], P('fsdp'), may hold values from -4 to 4
- v_bias: bfloat16 [768], P('fsdp'), may hold values from -0.75 to 0.75
- out_bias: bfloat16 [768], P('fsdp'), may hold values from -4 to 4
- ln2_gain: bfloat16 [768], P('fsdp'), may hold values from 0.5 to 1.5
- ln2_bias: bfloat16 [768], P('fsdp'), may hold values from -3 to 3
- up_bias: bfloat16 [3072], P('fsdp'), may hold values from -6 to 6
- down_bias: bfloat16 [768], P('fsdp'), may hold values from -4 to 4
- cotangent: bfloat16 [8, 2048, 768], P(('dp', 'fsdp'), 'ctx'), may hold values from -6 to 6
Outputs:
- output: bfloat16 [8, 2048, 768], P(('dp', 'fsdp'), 'ctx')
- input_grad: bfloat16 [8, 2048, 768], P(('dp', 'fsdp'), 'ctx')
- w_qkv_grad: float32 [768, 2304], P('fsdp')
- w_out_grad: float32 [768, 768], P('fsdp')
- w_up_grad: float32 [768, 3072], P('fsdp')
- w_down_grad: float32 [3072, 768], P('fsdp')
- ln1_gain_grad: float32 [768], P('fsdp')
- ln1_bias_grad: float32 [768], P('fsdp')
- q_bias_grad: float32 [768], P('fsdp')
- v_bias_grad: float32 [768], P('fsdp')
- out_bias_grad: float32 [768], P('fsdp')
- ln2_gain_grad: float32 [768], P('fsdp')
- ln2_bias_grad: float32 [768], P('fsdp')
- up_bias_grad: float32 [3072], P('fsdp')
- down_bias_grad: float32 [768], P('fsdp')
All inputs are finite; a program needn't handle non-finite values.
Results may differ from a plain program's by a relative error of at most 0.018.
Values may be sent and summed in bfloat16 or wider, within the bound.
A program may use at most 192 MiB of HBM per device.

v0:
```python
import math

import jax
import jax.numpy as jnp
from jax import lax
from jax.sharding import PartitionSpec as P

H = 12
HD = 64


norm_eps = 1e-05
masked_fill = -1e30


def from_behind(value, axis, by):
    size = lax.axis_size(axis)
    return lax.ppermute(value, axis, [(i, (i + by) % size) for i in range(size)])


def from_behind_2(block, axis, distance):
    devices = range(lax.axis_size(axis))
    route = [(i - distance, i) for i in devices if i - distance in devices]
    return lax.ppermute(block, axis, route)


def layer_norm(values, gain, shift):
    average = jnp.mean(values, axis=-1, keepdims=True)
    centred = values - average
    spread = jnp.mean(centred * centred, axis=-1, keepdims=True)
    return centred * lax.rsqrt(spread + norm_eps) * gain + shift


def exact_gelu(values):
    return jax.nn.gelu(values, approximate=False)


def split_heads(array):
    return array.reshape(array.shape[0], array.shape[1], H, HD)


def allowed_mask(query_start, query_count, key_start, key_count):
    rows = query_start + jnp.arange(query_count, dtype=jnp.int32)
    columns = key_start + jnp.arange(key_count, dtype=jnp.int32)
    return (columns[None, :] <= rows[:, None])[None, :, None, :]


def fold_keys(query_heads, query_start, carry, pieces):
    query_count = query_heads.shape[1]
    keys, values = pieces
    length = keys.shape[1]
    step = math.gcd(length, 512)

    def one_part(index, state):
        highest, total, accum = state
        offset = index * step
        key_part = split_heads(lax.dynamic_slice_in_dim(keys, offset, step, 1))
        value_part = split_heads(lax.dynamic_slice_in_dim(values, offset, step, 1))
        scores = jnp.einsum(
            "sqhe,skhe->sqhk", query_heads, key_part, preferred_element_type=jnp.float32
        )
        allowed = allowed_mask(query_start, query_count, offset, step)
        new_high = jnp.maximum(highest, jnp.max(jnp.where(allowed, scores, masked_fill), axis=-1))
        weights = jnp.where(allowed, jnp.exp(scores - new_high[..., None]), 0.0)
        factor = jnp.exp(highest - new_high)
        total = total * factor + jnp.sum(weights, axis=-1)
        accum = accum * factor[..., None] + jnp.einsum(
            "sqhk,skhe->sqhe",
            weights.astype(jnp.bfloat16),
            value_part,
            preferred_element_type=jnp.float32,
        )
        return (new_high, total, accum)

    return lax.fori_loop(0, length // step, one_part, carry)


def block_grads(queries, upstream, log_total, delta, keys, values, query_start, key_start):
    seqs, query_count, width = queries.shape
    key_count = keys.shape[1]
    query_heads = split_heads(queries)
    upstream_heads = split_heads(upstream)
    key_heads = split_heads(keys)
    value_heads = split_heads(values)
    scores = jnp.einsum(
        "sqhe,skhe->sqhk", query_heads, key_heads, preferred_element_type=jnp.float32
    )
    allowed = allowed_mask(query_start, query_count, key_start, key_count)
    weights = jnp.where(allowed, jnp.exp(scores - log_total[..., None]), 0.0)
    value_part = jnp.einsum(
        "sqhk,sqhe->skhe",
        weights.astype(jnp.bfloat16),
        upstream_heads,
        preferred_element_type=jnp.float32,
    )
    weight_grad = jnp.einsum(
        "sqhe,skhe->sqhk", upstream_heads, value_heads, preferred_element_type=jnp.float32
    )
    score_low = (weights * (weight_grad - delta[..., None])).astype(jnp.bfloat16)
    query_part = jnp.einsum(
        "sqhk,skhe->sqhe", score_low, key_heads, preferred_element_type=jnp.float32
    )
    key_part = jnp.einsum(
        "sqhk,sqhe->skhe", score_low, query_heads, preferred_element_type=jnp.float32
    )
    return (
        query_part.reshape(seqs, query_count, width),
        key_part.reshape(seqs, key_count, width),
        value_part.reshape(seqs, key_count, width),
    )


def per_device(
    inputs,
    w_qkv,
    w_out,
    w_up,
    w_down,
    ln1_gain,
    ln1_bias,
    q_bias,
    v_bias,
    out_bias,
    ln2_gain,
    ln2_bias,
    up_bias,
    down_bias,
    cotangent,
):
    gathered = (
        lax.all_gather(w_qkv, "fsdp", axis=0, tiled=True),
        lax.all_gather(w_out, "fsdp", axis=0, tiled=True),
        lax.all_gather(w_up, "fsdp", axis=0, tiled=True),
        lax.all_gather(w_down, "fsdp", axis=0, tiled=True),
        lax.all_gather(ln1_gain, "fsdp", axis=0, tiled=True),
        lax.all_gather(ln1_bias, "fsdp", axis=0, tiled=True),
        lax.all_gather(q_bias, "fsdp", axis=0, tiled=True),
        lax.all_gather(v_bias, "fsdp", axis=0, tiled=True),
        lax.all_gather(out_bias, "fsdp", axis=0, tiled=True),
        lax.all_gather(ln2_gain, "fsdp", axis=0, tiled=True),
        lax.all_gather(ln2_bias, "fsdp", axis=0, tiled=True),
        lax.all_gather(up_bias, "fsdp", axis=0, tiled=True),
        lax.all_gather(down_bias, "fsdp", axis=0, tiled=True),
    )
    (
        qkv_full,
        out_full,
        up_full,
        down_full,
        gain_one,
        shift_one,
        query_shift,
        value_shift,
        branch_shift,
        gain_two,
        shift_two,
        hidden_shift,
        final_shift,
    ) = gathered
    seqs, block, width = inputs.shape
    tokens = seqs * block
    scale = HD ** (-0.5)
    members = lax.axis_size("ctx")
    place = lax.axis_index("ctx")
    my_start = place * block
    flat_in = inputs.reshape(tokens, width).astype(jnp.float32)
    normed1, norm1_pull = jax.vjp(
        layer_norm, flat_in, gain_one.astype(jnp.float32), shift_one.astype(jnp.float32)
    )
    normed1_low = normed1.astype(jnp.bfloat16)
    projected = jnp.dot(normed1_low, qkv_full, preferred_element_type=jnp.float32)
    queries = (
        ((projected[:, :width] + query_shift.astype(jnp.float32)) * scale)
        .astype(jnp.bfloat16)
        .reshape(seqs, block, width)
    )
    keys = projected[:, width : 2 * width].astype(jnp.bfloat16).reshape(seqs, block, width)
    values = (
        (projected[:, 2 * width :] + value_shift.astype(jnp.float32))
        .astype(jnp.bfloat16)
        .reshape(seqs, block, width)
    )
    start_state = (
        jnp.full((seqs, block, H), masked_fill, jnp.float32),
        jnp.zeros((seqs, block, H), jnp.float32),
        jnp.zeros((seqs, block, H, HD), jnp.float32),
    )
    highest, total, accum = fold_keys(
        split_heads(queries),
        my_start,
        start_state,
        (
            lax.all_gather(keys, "ctx", axis=1, tiled=True),
            lax.all_gather(values, "ctx", axis=1, tiled=True),
        ),
    )
    attended = accum / total[..., None]
    log_total = highest + jnp.log(total)
    attended_low = attended.reshape(tokens, width).astype(jnp.bfloat16)
    middle = (
        flat_in
        + jnp.dot(attended_low, out_full, preferred_element_type=jnp.float32)
        + branch_shift.astype(jnp.float32)
    )
    normed2, norm2_pull = jax.vjp(
        layer_norm, middle, gain_two.astype(jnp.float32), shift_two.astype(jnp.float32)
    )
    normed2_low = normed2.astype(jnp.bfloat16)
    hidden = jnp.dot(
        normed2_low, up_full, preferred_element_type=jnp.float32
    ) + hidden_shift.astype(jnp.float32)
    activated, gelu_pull = jax.vjp(exact_gelu, hidden)
    activated_low = activated.astype(jnp.bfloat16)
    output = (
        middle
        + jnp.dot(activated_low, down_full, preferred_element_type=jnp.float32)
        + final_shift.astype(jnp.float32)
    )
    result = output.astype(jnp.bfloat16).reshape(seqs, block, width)
    upstream_low = cotangent.reshape(tokens, width)
    upstream = upstream_low.astype(jnp.float32)
    down_grad = jnp.einsum(
        "rf,rd->fd", activated_low, upstream_low, preferred_element_type=jnp.float32
    )
    final_shift_grad = jnp.sum(upstream, axis=0)
    activated_grad = jnp.einsum(
        "rd,fd->rf", upstream_low, down_full, preferred_element_type=jnp.float32
    )
    hidden_low = gelu_pull(activated_grad)[0].astype(jnp.bfloat16)
    up_grad = jnp.einsum("rd,rf->df", normed2_low, hidden_low, preferred_element_type=jnp.float32)
    hidden_shift_grad = jnp.sum(hidden_low.astype(jnp.float32), axis=0)
    normed2_grad = jnp.einsum("rf,df->rd", hidden_low, up_full, preferred_element_type=jnp.float32)
    middle_part, gain_two_grad, shift_two_grad = norm2_pull(normed2_grad)
    middle_grad = upstream + middle_part
    branch_low = middle_grad.astype(jnp.bfloat16)
    branch_shift_grad = jnp.sum(branch_low.astype(jnp.float32), axis=0)
    out_grad = jnp.einsum("rd,re->de", attended_low, branch_low, preferred_element_type=jnp.float32)
    attended_grad = (
        jnp.einsum("re,de->rd", branch_low, out_full, preferred_element_type=jnp.float32)
        .astype(jnp.bfloat16)
        .reshape(seqs, block, width)
    )
    delta = jnp.sum(split_heads(attended_grad).astype(jnp.float32) * attended, axis=-1)
    zeros = jnp.zeros((seqs, block, width), jnp.float32)

    def key_turn(step, state):
        moving_keys, moving_values, key_acc, value_acc, query_acc = state
        source = (place - step) % members
        part_q, part_k, part_v = block_grads(
            queries,
            attended_grad,
            log_total,
            delta,
            moving_keys,
            moving_values,
            my_start,
            source * block,
        )
        key_acc, value_acc = (
            from_behind((key_acc + part_k).astype(jnp.bfloat16), "ctx", 1).astype(jnp.float32),
            from_behind((value_acc + part_v).astype(jnp.bfloat16), "ctx", 1).astype(jnp.float32),
        )
        moving_keys, moving_values = from_behind_2((moving_keys, moving_values), "ctx", 1)
        return (moving_keys, moving_values, key_acc, value_acc, query_acc + part_q)

    state = lax.fori_loop(0, members, key_turn, (keys, values, zeros, zeros, zeros))
    key_acc, value_acc, query_acc = (state[2], state[3], state[4])
    query_pre = (
        (query_acc.astype(jnp.bfloat16).astype(jnp.float32) * scale)
        .astype(jnp.bfloat16)
        .reshape(tokens, width)
    )
    key_low = key_acc.astype(jnp.bfloat16).reshape(tokens, width)
    value_low = value_acc.astype(jnp.bfloat16).reshape(tokens, width)
    stacked = jnp.concatenate([query_pre, key_low, value_low], axis=1)
    qkv_grad = jnp.einsum("rd,rf->df", normed1_low, stacked, preferred_element_type=jnp.float32)
    query_shift_grad = jnp.sum(query_pre.astype(jnp.float32), axis=0)
    value_shift_grad = jnp.sum(value_low.astype(jnp.float32), axis=0)
    normed1_grad = jnp.einsum("rf,df->rd", stacked, qkv_full, preferred_element_type=jnp.float32)
    input_part, gain_one_grad, shift_one_grad = norm1_pull(normed1_grad)
    input_grad = (middle_grad + input_part).astype(jnp.bfloat16).reshape(seqs, block, width)
    shared = (
        lax.psum_scatter(
            qkv_grad.astype(jnp.bfloat16), "fsdp", scatter_dimension=0, tiled=True
        ).astype(jnp.float32),
        lax.psum_scatter(
            out_grad.astype(jnp.bfloat16), "fsdp", scatter_dimension=0, tiled=True
        ).astype(jnp.float32),
        lax.psum_scatter(
            up_grad.astype(jnp.bfloat16), "fsdp", scatter_dimension=0, tiled=True
        ).astype(jnp.float32),
        lax.psum_scatter(
            down_grad.astype(jnp.bfloat16), "fsdp", scatter_dimension=0, tiled=True
        ).astype(jnp.float32),
        lax.psum_scatter(
            gain_one_grad.astype(jnp.bfloat16), "fsdp", scatter_dimension=0, tiled=True
        ).astype(jnp.float32),
        lax.psum_scatter(
            shift_one_grad.astype(jnp.bfloat16), "fsdp", scatter_dimension=0, tiled=True
        ).astype(jnp.float32),
        lax.psum_scatter(
            query_shift_grad.astype(jnp.bfloat16), "fsdp", scatter_dimension=0, tiled=True
        ).astype(jnp.float32),
        lax.psum_scatter(
            value_shift_grad.astype(jnp.bfloat16), "fsdp", scatter_dimension=0, tiled=True
        ).astype(jnp.float32),
        lax.psum_scatter(
            branch_shift_grad.astype(jnp.bfloat16), "fsdp", scatter_dimension=0, tiled=True
        ).astype(jnp.float32),
        lax.psum_scatter(
            gain_two_grad.astype(jnp.bfloat16), "fsdp", scatter_dimension=0, tiled=True
        ).astype(jnp.float32),
        lax.psum_scatter(
            shift_two_grad.astype(jnp.bfloat16), "fsdp", scatter_dimension=0, tiled=True
        ).astype(jnp.float32),
        lax.psum_scatter(
            hidden_shift_grad.astype(jnp.bfloat16), "fsdp", scatter_dimension=0, tiled=True
        ).astype(jnp.float32),
        lax.psum_scatter(
            final_shift_grad.astype(jnp.bfloat16), "fsdp", scatter_dimension=0, tiled=True
        ).astype(jnp.float32),
    )
    (
        share_qkv,
        share_out,
        share_up,
        share_down,
        share_gain_one,
        share_shift_one,
        share_query,
        share_value,
        share_branch,
        share_gain_two,
        share_shift_two,
        share_hidden,
        share_final,
    ) = shared
    totals = lax.psum(
        (
            share_qkv,
            share_out,
            share_up,
            share_down,
            share_gain_one,
            share_shift_one,
            share_query,
            share_value,
            share_branch,
            share_gain_two,
            share_shift_two,
            share_hidden,
            share_final,
        ),
        ("dp", "ctx"),
    )
    return (
        result,
        input_grad,
        totals[0],
        totals[1],
        totals[2],
        totals[3],
        totals[4],
        totals[5],
        totals[6],
        totals[7],
        totals[8],
        totals[9],
        totals[10],
        totals[11],
        totals[12],
    )


def solution(mesh):
    return jax.shard_map(
        per_device,
        mesh=mesh,
        in_specs=(
            P(("dp", "fsdp"), "ctx", None),
            P("fsdp", None),
            P("fsdp", None),
            P("fsdp", None),
            P("fsdp", None),
            P("fsdp"),
            P("fsdp"),
            P("fsdp"),
            P("fsdp"),
            P("fsdp"),
            P("fsdp"),
            P("fsdp"),
            P("fsdp"),
            P("fsdp"),
            P(("dp", "fsdp"), "ctx", None),
        ),
        out_specs=(
            P(("dp", "fsdp"), "ctx", None),
            P(("dp", "fsdp"), "ctx", None),
            P("fsdp", None),
            P("fsdp", None),
            P("fsdp", None),
            P("fsdp", None),
            P("fsdp"),
            P("fsdp"),
            P("fsdp"),
            P("fsdp"),
            P("fsdp"),
            P("fsdp"),
            P("fsdp"),
            P("fsdp"),
            P("fsdp"),
        ),
        check_vma=False,
    )
```

profile of v0, /device:TPU:1, one launch (start us, length us, event | category | flops | bytes accessed | tf_op | source)
XLA Modules:
  0.0 1277.2 jit_solution(5903340607072337274)
XLA Ops:
  18.4 42.6 %all-gather.16.cloned.1.call-done = bf16[768,2304]{1,0:T(8,128)(2,1)} async-done(((bf16[384,2304]{1,0:T(8,128)(2,1)}), bf16[768,2304]{1,0:T(8,128)(2,1)}) %all-gather.16.cloned.1.call-update) | async-done | bytes 3538960 | tf_op jit(solution)/shard_map/all_gather | solution.py:131
  97.9 36.4 %all-gather.18.cloned.1.call-done = bf16[2,2048,768]{1,2,0:T(8,128)(2,1)} async-done(((bf16[2,256,768]{1,2,0:T(8,128)(2,1)}), bf16[2,2048,768]{1,2,0:T(8,128)(2,1)}) %all-gather.18.cloned.1.call-update) | async-done | bytes 6291472 | tf_op jit(solution)/shard_map/all_gather | solution.py:193
  134.3 65.0 %all-gather.20.cloned.1.call-done = bf16[2,2048,768]{1,2,0:T(8,128)(2,1)} async-done(((bf16[2,256,768]{1,2,0:T(8,128)(2,1)}), bf16[2,2048,768]{1,2,0:T(8,128)(2,1)}) %all-gather.20.cloned.1.call-update) | async-done | bytes 6291472 | tf_op jit(solution)/shard_map/all_gather | solution.py:194
  199.3 80.7 %while.43 = (s32[]{:T(128)}, f32[2,256,12]{1,2,0:T(8,128)S(1)}, f32[2,256,12]{1,2,0:T(8,128)S(1)}, f32[2,256,12,64]{1,3,2,0:T(8,128)S(1)}, s32[]{:T(128)}, /*ind...) while((s32[]{:T(128)}, f32[2,256,12]{1,2,0:T(8,128)S(1)}, ...), condition=%wide.region_5.6_spmd.clone, body=%wide.region_2.5_spmd.clone.sunk | while | flops 831814400 | bytes 105519352 | solution.py:75
  201.6 6.7 fusion.146
  208.3 6.8 fusion.147
  221.4 6.5 fusion.146
  227.9 8.5 fusion.147
  243.3 6.5 fusion.146
  249.8 6.8 fusion.147
  262.8 6.5 fusion.146
  269.3 6.8 fusion.147
  285.6 7.3 fusion.61
  292.9 56.5 %all-gather.26.cloned.1.call-done = bf16[3072,768]{1,0:T(8,128)(2,1)} async-done(((bf16[1536,768]{1,0:T(8,128)(2,1)}), bf16[3072,768]{1,0:T(8,128)(2,1)}) %all-gather.26.cloned.1.call-update) | async-done | bytes 4718608 | tf_op jit(solution)/shard_map/all_gather | solution.py:134
  349.4 20.0 %fusion.63 = (bf16[3072]{0:T(1024)(128)(2,1)S(1)}, bf16[512,3072]{1,0:T(8,128)(2,1)S(1)}, f32[512,3072]{1,0:T(8,128)}) fusion(f32[512,3072]{1,0:T(8,128)} %fusion.61, f32[3072]{0:T(1024)S(1)} %bitcast.217, bf16[512,768]{1,0:T(8,128)(2,1)S(1)} %bitcast.203, bf16[3072,768]{1,0:T(8,128)(2,1)} %all-gather.26.cloned.1.call-done), kind=kOutput, calls=%fused_computation.141 | convolution fusion | flops 2532307968 | bytes 21252096 | tf_op jit(solution)/shard_map/rd,fd->rf/dot_general | solution.py:226
  384.9 400.6 %while.44 = (s32[]{:T(128)}, bf16[2,256,768]{1,2,0:T(8,128)(2,1)}, bf16[2,256,768]{1,2,0:T(8,128)(2,1)}, f32[2,256,768]{1,2,0:T(8,128)}, f32[2,256,768]{1,2,0:T(...) while((s32[]{:T(128)}, bf16[2,256,768]{1,2,0:T(8,128)(2,1)}, ...), condition=%wide.wide.region_12.13_spmd.clone, body=%wide.wide.region_11.12_spmd.clone.sunk | while | flops 1023214080 | bytes 103297680 | solution.py:266
  426.1 8.4 collective-permute-done.1
  470.2 6.0 collective-permute-done
  476.2 8.4 collective-permute-done.1
  526.4 8.4 collective-permute-done.1
  576.5 8.4 collective-permute-done.1
  620.6 6.0 collective-permute-done
  626.6 8.4 collective-permute-done.1
  676.8 8.4 collective-permute-done.1
  726.9 8.4 collective-permute-done.1
  777.0 8.4 collective-permute-done.1
  797.4 6.5 convolution_convert_fusion.1
  804.3 6.4 multiply_convert_fusion
  830.2 7.3 all-reduce.10
  846.9 61.3 %reduce-scatter.9.cloned.1.call-done = bf16[384,3072]{1,0:T(8,128)(2,1)} async-done(((bf16[768,3072]{1,0:T(8,128)(2,1)}), bf16[384,3072]{1,0:T(8,128)(2,1)}) %reduce-scatter.9.cloned.1.call-update) | async-done | bytes 2359312 | tf_op jit(solution)/shard_map/reduce_scatter | solution.py:289
  908.2 62.9 %reduce-scatter.11.cloned.1.call-done = bf16[1536,768]{1,0:T(8,128)(2,1)} async-done(((bf16[3072,768]{1,0:T(8,128)(2,1)}), bf16[1536,768]{1,0:T(8,128)(2,1)}) %reduce-scatter.11.cloned.1.call-update) | async-done | bytes 2359312 | tf_op jit(solution)/shard_map/reduce_scatter | solution.py:292
  971.1 298.8 %all-reduce.12 = (f32[384,2304]{1,0:T(8,128)}, f32[384,768]{1,0:T(8,128)}, f32[384,3072]{1,0:T(8,128)}, f32[1536,768]{1,0:T(8,128)}, f32[384]{0:T(512)}, /*index...) all-reduce(bf16[384,2304]{1,0:T(8,128)(2,1)} %reduce-scatter.5.clon, ...), channel_id=1, replica_groups=mesh['dp'=2,'ctx'=8,'fsdp'=2] {'dp','ctx'}, use_global_device_ids=true, to_apply=%region_16.17 | all-reduce | flops 3543552 | bytes 21270528 | tf_op jit(solution)/shard_map/psum | solution.py:338
  (532 shorter events, 453.3 us)
Async XLA Ops:
  7.2 53.9 %all-gather.16.cloned.1.call-start = ((), (), s32[]{:S(2)}) async-start(), calls=%async_computation.4 | async-start | bytes 5308416 | tf_op jit(solution)/shard_map/all_gather | solution.py:131
  7.9 126.4 %all-gather.18.cloned.1.call-start = ((), (), s32[]{:S(2)}) async-start(), calls=%async_computation.5 | async-start | bytes 7077888 | tf_op jit(solution)/shard_map/all_gather | solution.py:193
  68.5 130.7 %all-gather.20.cloned.1.call-start = ((), (), s32[]{:S(2)}) async-start(), calls=%async_computation.6 | async-start | bytes 7077888 | tf_op jit(solution)/shard_map/all_gather | solution.py:194
  78.6 204.4 %all-gather.22.cloned.1.call-start = ((), (), s32[]{:S(2)}) async-start(), calls=%async_computation.7 | async-start | bytes 1769472 | tf_op jit(solution)/shard_map/all_gather | solution.py:132
  79.2 206.3 %all-gather.24.cloned.1.call-start = ((), (), s32[]{:S(2)}) async-start(), calls=%async_computation.8 | async-start | bytes 7077888 | tf_op jit(solution)/shard_map/all_gather | solution.py:133
  79.8 269.6 %all-gather.26.cloned.1.call-start = ((), (), s32[]{:S(2)}) async-start(), calls=%async_computation.9 | async-start | bytes 7077888 | tf_op jit(solution)/shard_map/all_gather | solution.py:134
  80.4 766.5 %reduce-scatter.7.cloned.1.call-start = ((), (), s32[]{:S(2)}) async-start(), calls=%async_computation.11 | async-start | bytes 1769472 | tf_op jit(solution)/shard_map/reduce_scatter | solution.py:286
  384.8 462.1 %reduce-scatter.5.cloned.1.call-start = ((), (), s32[]{:S(2)}) async-start(), calls=%async_computation.10 | async-start | bytes 5308416 | tf_op jit(solution)/shard_map/reduce_scatter | solution.py:283
  402.2 15.4 %collective-permute-start.3 = (bf16[2,256,768]{1,2,0:T(8,128)(2,1)}, bf16[2,256,768]{1,2,0:T(8,128)(2,1)}, u32[]{:S(2)}, u32[]{:S(2)}) collective-permute-start(bf16[2,256,768]{1,2,0:T(8,128)(2,1)} %fusion.164), channel_id=1, source_target_pairs={{0,2},{2,4},{4,6},{6,8},{8,10},{10,12},{12,14},{14,0},{1,3},{3,5},... | collective-permute-start | bytes 2359304 | tf_op jit(solution)/shard_map/while/body/eval_jaxpr/ppermute | solution.py:18
  402.5 23.6 %collective-permute-start = (bf16[2,256,768]{1,2,0:T(8,128)(2,1)}, bf16[2,256,768]{1,2,0:T(8,128)(2,1)}, u32[]{:S(2)}, u32[]{:S(2)}) collective-permute-start(bf16[2,256,768]{1,2,0:T(8,128)(2,1)} %copy.138), channel_id=1, source_target_pairs={{0,2},{2,4},{4,6},{6,8},{8,10},{10,12},{12,14},{1,3},{3,5},{5,7},{... | collective-permute-start | bytes 2359304 | tf_op jit(solution)/shard_map/while/body/eval_jaxpr/ppermute | solution.py:24
  405.7 28.8 %collective-permute-start.1 = (bf16[2,256,768]{1,2,0:T(8,128)(2,1)}, bf16[2,256,768]{1,2,0:T(8,128)(2,1)}, u32[]{:S(2)}, u32[]{:S(2)}) collective-permute-start(bf16[2,256,768]{1,2,0:T(8,128)(2,1)} %copy.139), channel_id=1, source_target_pairs={{0,2},{2,4},{4,6},{6,8},{8,10},{10,12},{12,14},{1,3},{3,5},{5,7},{... | collective-permute-start | bytes 2359304 | tf_op jit(solution)/shard_map/while/body/eval_jaxpr/ppermute | solution.py:24
  452.3 15.4 %collective-permute-start.3 = (bf16[2,256,768]{1,2,0:T(8,128)(2,1)}, bf16[2,256,768]{1,2,0:T(8,128)(2,1)}, u32[]{:S(2)}, u32[]{:S(2)}) collective-permute-start(bf16[2,256,768]{1,2,0:T(8,128)(2,1)} %fusion.164), channel_id=1, source_target_pairs={{0,2},{2,4},{4,6},{6,8},{8,10},{10,12},{12,14},{14,0},{1,3},{3,5},... | collective-permute-start | bytes 2359304 | tf_op jit(solution)/shard_map/while/body/eval_jaxpr/ppermute | solution.py:18
  452.6 23.6 %collective-permute-start = (bf16[2,256,768]{1,2,0:T(8,128)(2,1)}, bf16[2,256,768]{1,2,0:T(8,128)(2,1)}, u32[]{:S(2)}, u32[]{:S(2)}) collective-permute-start(bf16[2,256,768]{1,2,0:T(8,128)(2,1)} %copy.138), channel_id=1, source_target_pairs={{0,2},{2,4},{4,6},{6,8},{8,10},{10,12},{12,14},{1,3},{3,5},{5,7},{... | collective-permute-start | bytes 2359304 | tf_op jit(solution)/shard_map/while/body/eval_jaxpr/ppermute | solution.py:24
  455.8 28.8 %collective-permute-start.1 = (bf16[2,256,768]{1,2,0:T(8,128)(2,1)}, bf16[2,256,768]{1,2,0:T(8,128)(2,1)}, u32[]{:S(2)}, u32[]{:S(2)}) collective-permute-start(bf16[2,256,768]{1,2,0:T(8,128)(2,1)} %copy.139), channel_id=1, source_target_pairs={{0,2},{2,4},{4,6},{6,8},{8,10},{10,12},{12,14},{1,3},{3,5},{5,7},{... | collective-permute-start | bytes 2359304 | tf_op jit(solution)/shard_map/while/body/eval_jaxpr/ppermute | solution.py:24
  502.5 15.4 %collective-permute-start.3 = (bf16[2,256,768]{1,2,0:T(8,128)(2,1)}, bf16[2,256,768]{1,2,0:T(8,128)(2,1)}, u32[]{:S(2)}, u32[]{:S(2)}) collective-permute-start(bf16[2,256,768]{1,2,0:T(8,128)(2,1)} %fusion.164), channel_id=1, source_target_pairs={{0,2},{2,4},{4,6},{6,8},{8,10},{10,12},{12,14},{14,0},{1,3},{3,5},... | collective-permute-start | bytes 2359304 | tf_op jit(solution)/shard_map/while/body/eval_jaxpr/ppermute | solution.py:18
  502.8 23.6 %collective-permute-start = (bf16[2,256,768]{1,2,0:T(8,128)(2,1)}, bf16[2,256,768]{1,2,0:T(8,128)(2,1)}, u32[]{:S(2)}, u32[]{:S(2)}) collective-permute-start(bf16[2,256,768]{1,2,0:T(8,128)(2,1)} %copy.138), channel_id=1, source_target_pairs={{0,2},{2,4},{4,6},{6,8},{8,10},{10,12},{12,14},{1,3},{3,5},{5,7},{... | collective-permute-start | bytes 2359304 | tf_op jit(solution)/shard_map/while/body/eval_jaxpr/ppermute | solution.py:24
  506.0 28.8 %collective-permute-start.1 = (bf16[2,256,768]{1,2,0:T(8,128)(2,1)}, bf16[2,256,768]{1,2,0:T(8,128)(2,1)}, u32[]{:S(2)}, u32[]{:S(2)}) collective-permute-start(bf16[2,256,768]{1,2,0:T(8,128)(2,1)} %copy.139), channel_id=1, source_target_pairs={{0,2},{2,4},{4,6},{6,8},{8,10},{10,12},{12,14},{1,3},{3,5},{5,7},{... | collective-permute-start | bytes 2359304 | tf_op jit(solution)/shard_map/while/body/eval_jaxpr/ppermute | solution.py:24
  552.6 15.4 %collective-permute-start.3 = (bf16[2,256,768]{1,2,0:T(8,128)(2,1)}, bf16[2,256,768]{1,2,0:T(8,128)(2,1)}, u32[]{:S(2)}, u32[]{:S(2)}) collective-permute-start(bf16[2,256,768]{1,2,0:T(8,128)(2,1)} %fusion.164), channel_id=1, source_target_pairs={{0,2},{2,4},{4,6},{6,8},{8,10},{10,12},{12,14},{14,0},{1,3},{3,5},... | collective-permute-start | bytes 2359304 | tf_op jit(solution)/shard_map/while/body/eval_jaxpr/ppermute | solution.py:18
  552.9 23.6 %collective-permute-start = (bf16[2,256,768]{1,2,0:T(8,128)(2,1)}, bf16[2,256,768]{1,2,0:T(8,128)(2,1)}, u32[]{:S(2)}, u32[]{:S(2)}) collective-permute-start(bf16[2,256,768]{1,2,0:T(8,128)(2,1)} %copy.138), channel_id=1, source_target_pairs={{0,2},{2,4},{4,6},{6,8},{8,10},{10,12},{12,14},{1,3},{3,5},{5,7},{... | collective-permute-start | bytes 2359304 | tf_op jit(solution)/shard_map/while/body/eval_jaxpr/ppermute | solution.py:24
  556.1 28.8 %collective-permute-start.1 = (bf16[2,256,768]{1,2,0:T(8,128)(2,1)}, bf16[2,256,768]{1,2,0:T(8,128)(2,1)}, u32[]{:S(2)}, u32[]{:S(2)}) collective-permute-start(bf16[2,256,768]{1,2,0:T(8,128)(2,1)} %copy.139), channel_id=1, source_target_pairs={{0,2},{2,4},{4,6},{6,8},{8,10},{10,12},{12,14},{1,3},{3,5},{5,7},{... | collective-permute-start | bytes 2359304 | tf_op jit(solution)/shard_map/while/body/eval_jaxpr/ppermute | solution.py:24
  603.1 23.6 %collective-permute-start = (bf16[2,256,768]{1,2,0:T(8,128)(2,1)}, bf16[2,256,768]{1,2,0:T(8,128)(2,1)}, u32[]{:S(2)}, u32[]{:S(2)}) collective-permute-start(bf16[2,256,768]{1,2,0:T(8,128)(2,1)} %copy.138), channel_id=1, source_target_pairs={{0,2},{2,4},{4,6},{6,8},{8,10},{10,12},{12,14},{1,3},{3,5},{5,7},{... | collective-permute-start | bytes 2359304 | tf_op jit(solution)/shard_map/while/body/eval_jaxpr/ppermute | solution.py:24
  606.3 28.8 %collective-permute-start.1 = (bf16[2,256,768]{1,2,0:T(8,128)(2,1)}, bf16[2,256,768]{1,2,0:T(8,128)(2,1)}, u32[]{:S(2)}, u32[]{:S(2)}) collective-permute-start(bf16[2,256,768]{1,2,0:T(8,128)(2,1)} %copy.139), channel_id=1, source_target_pairs={{0,2},{2,4},{4,6},{6,8},{8,10},{10,12},{12,14},{1,3},{3,5},{5,7},{... | collective-permute-start | bytes 2359304 | tf_op jit(solution)/shard_map/while/body/eval_jaxpr/ppermute | solution.py:24
  652.9 15.4 %collective-permute-start.3 = (bf16[2,256,768]{1,2,0:T(8,128)(2,1)}, bf16[2,256,768]{1,2,0:T(8,128)(2,1)}, u32[]{:S(2)}, u32[]{:S(2)}) collective-permute-start(bf16[2,256,768]{1,2,0:T(8,128)(2,1)} %fusion.164), channel_id=1, source_target_pairs={{0,2},{2,4},{4,6},{6,8},{8,10},{10,12},{12,14},{14,0},{1,3},{3,5},... | collective-permute-start | bytes 2359304 | tf_op jit(solution)/shard_map/while/body/eval_jaxpr/ppermute | solution.py:18
  653.2 23.6 %collective-permute-start = (bf16[2,256,768]{1,2,0:T(8,128)(2,1)}, bf16[2,256,768]{1,2,0:T(8,128)(2,1)}, u32[]{:S(2)}, u32[]{:S(2)}) collective-permute-start(bf16[2,256,768]{1,2,0:T(8,128)(2,1)} %copy.138), channel_id=1, source_target_pairs={{0,2},{2,4},{4,6},{6,8},{8,10},{10,12},{12,14},{1,3},{3,5},{5,7},{... | collective-permute-start | bytes 2359304 | tf_op jit(solution)/shard_map/while/body/eval_jaxpr/ppermute | solution.py:24
  656.4 28.8 %collective-permute-start.1 = (bf16[2,256,768]{1,2,0:T(8,128)(2,1)}, bf16[2,256,768]{1,2,0:T(8,128)(2,1)}, u32[]{:S(2)}, u32[]{:S(2)}) collective-permute-start(bf16[2,256,768]{1,2,0:T(8,128)(2,1)} %copy.139), channel_id=1, source_target_pairs={{0,2},{2,4},{4,6},{6,8},{8,10},{10,12},{12,14},{1,3},{3,5},{5,7},{... | collective-permute-start | bytes 2359304 | tf_op jit(solution)/shard_map/while/body/eval_jaxpr/ppermute | solution.py:24
  703.3 23.6 %collective-permute-start = (bf16[2,256,768]{1,2,0:T(8,128)(2,1)}, bf16[2,256,768]{1,2,0:T(8,128)(2,1)}, u32[]{:S(2)}, u32[]{:S(2)}) collective-permute-start(bf16[2,256,768]{1,2,0:T(8,128)(2,1)} %copy.138), channel_id=1, source_target_pairs={{0,2},{2,4},{4,6},{6,8},{8,10},{10,12},{12,14},{1,3},{3,5},{5,7},{... | collective-permute-start | bytes 2359304 | tf_op jit(solution)/shard_map/while/body/eval_jaxpr/ppermute | solution.py:24
  706.5 28.8 %collective-permute-start.1 = (bf16[2,256,768]{1,2,0:T(8,128)(2,1)}, bf16[2,256,768]{1,2,0:T(8,128)(2,1)}, u32[]{:S(2)}, u32[]{:S(2)}) collective-permute-start(bf16[2,256,768]{1,2,0:T(8,128)(2,1)} %copy.139), channel_id=1, source_target_pairs={{0,2},{2,4},{4,6},{6,8},{8,10},{10,12},{12,14},{1,3},{3,5},{5,7},{... | collective-permute-start | bytes 2359304 | tf_op jit(solution)/shard_map/while/body/eval_jaxpr/ppermute | solution.py:24
  753.2 15.4 %collective-permute-start.3 = (bf16[2,256,768]{1,2,0:T(8,128)(2,1)}, bf16[2,256,768]{1,2,0:T(8,128)(2,1)}, u32[]{:S(2)}, u32[]{:S(2)}) collective-permute-start(bf16[2,256,768]{1,2,0:T(8,128)(2,1)} %fusion.164), channel_id=1, source_target_pairs={{0,2},{2,4},{4,6},{6,8},{8,10},{10,12},{12,14},{14,0},{1,3},{3,5},... | collective-permute-start | bytes 2359304 | tf_op jit(solution)/shard_map/while/body/eval_jaxpr/ppermute | solution.py:18
  753.5 23.6 %collective-permute-start = (bf16[2,256,768]{1,2,0:T(8,128)(2,1)}, bf16[2,256,768]{1,2,0:T(8,128)(2,1)}, u32[]{:S(2)}, u32[]{:S(2)}) collective-permute-start(bf16[2,256,768]{1,2,0:T(8,128)(2,1)} %copy.138), channel_id=1, source_target_pairs={{0,2},{2,4},{4,6},{6,8},{8,10},{10,12},{12,14},{1,3},{3,5},{5,7},{... | collective-permute-start | bytes 2359304 | tf_op jit(solution)/shard_map/while/body/eval_jaxpr/ppermute | solution.py:24
  756.7 28.8 %collective-permute-start.1 = (bf16[2,256,768]{1,2,0:T(8,128)(2,1)}, bf16[2,256,768]{1,2,0:T(8,128)(2,1)}, u32[]{:S(2)}, u32[]{:S(2)}) collective-permute-start(bf16[2,256,768]{1,2,0:T(8,128)(2,1)} %copy.139), channel_id=1, source_target_pairs={{0,2},{2,4},{4,6},{6,8},{8,10},{10,12},{12,14},{1,3},{3,5},{5,7},{... | collective-permute-start | bytes 2359304 | tf_op jit(solution)/shard_map/while/body/eval_jaxpr/ppermute | solution.py:24
  796.0 112.2 %reduce-scatter.9.cloned.1.call-start = ((), (), s32[]{:S(2)}) async-start(), calls=%async_computation.12 | async-start | bytes 7077888 | tf_op jit(solution)/shard_map/reduce_scatter | solution.py:289
  803.9 167.1 %reduce-scatter.11.cloned.1.call-start = ((), (), s32[]{:S(2)}) async-start(), calls=%async_computation.13 | async-start | bytes 7077888 | tf_op jit(solution)/shard_map/reduce_scatter | solution.py:292
  (111 other events, 1254.7 us)
Sparse Core Ops, SparseCore 0:
  9.6 51.4 all-gather.15
  68.6 65.5 all-gather.17
  135.9 63.3 all-gather.19
  200.7 20.5 all-gather.21
  222.6 62.6 all-gather.23
  286.7 62.6 all-gather.25
  384.9 21.7 reduce-scatter.6
  796.1 49.0 reduce-scatter.4
  848.1 59.9 reduce-scatter.8
  911.0 60.0 reduce-scatter.10
where the time goes:
time: 1280 us
  waiting for transfers between devices  478 us (37%)
  blocking collectives  338 us (26%)
  matrix products  188 us (15%)
  other arithmetic  116 us (9%)
  local copies, waits for them, and re-layouts  73.8 us (6%)
  starting transfers between devices  65.5 us (5%)
  between operations  16.7 us (1%)
    psum x1, blocking collectives, per_device(): lax.psum((share_qkv, share_out, share_up, share_down, share_gain_one, sha...  299 us
    ppermute x16, waiting for transfers between devices, from_behind_2(): return lax.ppermute(block, axis, route)  116 us
    all_gather x1, waiting for transfers between devices, per_device(): lax.all_gather(values, 'ctx', axis=1, tiled=True)  65 us
    reduce_scatter x1, waiting for transfers between devices, per_device(): lax.psum_scatter(down_grad.astype(jnp.bfloat16), 'fsdp', scatter_dimensio...  62.9 us
    reduce_scatter x1, waiting for transfers between devices, per_device(): lax.psum_scatter(up_grad.astype(jnp.bfloat16), 'fsdp', scatter_dimension=...  61.3 us
    all_gather x1, waiting for transfers between devices, per_device(): lax.all_gather(w_down, 'fsdp', axis=0, tiled=True)  56.5 us
    ppermute x16, starting transfers between devices, from_behind_2(): return lax.ppermute(block, axis, route)  43.3 us
    all_gather x1, waiting for transfers between devices, per_device(): lax.all_gather(w_qkv, 'fsdp', axis=0, tiled=True)  42.6 us
  transfers between devices with their start and end apart: 42, of which 30 were waited for; matrix products, arithmetic and copies ran while one was open for 25% of the time, Pallas kernels for 0%

commit v1 on v0

v1 whole, which is shorter than its diff:
```python
import math

import jax
import jax.numpy as jnp
from jax import lax
from jax.experimental import pallas as pl
from jax.experimental.pallas import tpu as pltpu
from jax.sharding import PartitionSpec as P

H = 12
HD = 64
F32 = jnp.float32
BF16 = jnp.bfloat16

norm_eps = 1e-05
masked_fill = -1e30
ROWS = 256
VMEM_LIMIT = 56 * 1024 * 1024


def layer_norm(values, gain, shift):
    average = jnp.mean(values, axis=-1, keepdims=True)
    centred = values - average
    spread = jnp.mean(centred * centred, axis=-1, keepdims=True)
    return centred * lax.rsqrt(spread + norm_eps) * gain + shift


def exact_gelu(values):
    return jax.nn.gelu(values, approximate=False)


def dot_nt(left, right):
    return lax.dot_general(left, right, (((1,), (1,)), ((), ())), preferred_element_type=F32)


def dot_tn(left, right):
    return lax.dot_general(left, right, (((0,), (0,)), ((), ())), preferred_element_type=F32)


def diagonal_mask(rows):
    keys = lax.broadcasted_iota(jnp.int32, (rows, rows), 0)
    queries = lax.broadcasted_iota(jnp.int32, (rows, rows), 1)
    return keys <= queries


def forward_kernel(q_ref, k_ref, v_ref, o_ref, log_ref):
    length = q_ref.shape[1]
    rows = math.gcd(length, ROWS)
    allowed = diagonal_mask(rows)
    for i in range(length // rows):
        here = pl.ds(i * rows, rows)
        queries = q_ref[0, here, :]
        near = jnp.where(allowed, dot_nt(k_ref[0, here, :], queries), masked_fill)
        high = jnp.max(near, axis=0, keepdims=True)
        if i:
            before = pl.ds(0, i * rows)
            far = dot_nt(k_ref[0, before, :], queries)
            high = jnp.maximum(high, jnp.max(far, axis=0, keepdims=True))
        near = jnp.exp(near - high)
        total = jnp.sum(near, axis=0, keepdims=True)
        accum = dot_tn(v_ref[0, here, :], near.astype(BF16))
        if i:
            far = jnp.exp(far - high)
            total = total + jnp.sum(far, axis=0, keepdims=True)
            accum = accum + dot_tn(v_ref[0, before, :], far.astype(BF16))
        o_ref[0, here, :] = (accum / total).T.astype(BF16)
        log_ref[0, :, here] = high + jnp.log(total)


def backward_kernel(
    q_ref, k_ref, v_ref, o_ref, log_ref, up_ref, dq_ref, dk_ref, dv_ref, dk_sum, dv_sum
):
    length = q_ref.shape[1]
    rows = math.gcd(length, ROWS)
    allowed = diagonal_mask(rows)
    for i in reversed(range(length // rows)):
        here = pl.ds(i * rows, rows)
        queries = q_ref[0, here, :]
        upstream = up_ref[0, here, :]
        log_total = log_ref[0, :, here]
        mixed = upstream.astype(F32) * o_ref[0, here, :].astype(F32)
        delta = jnp.sum(mixed.T, axis=0, keepdims=True)
        first = i == length // rows - 1

        def part(where, masked):
            keys = k_ref[0, where, :]
            probs = jnp.exp(dot_nt(keys, queries) - log_total)
            if masked:
                probs = jnp.where(allowed, probs, 0.0)
            prob_grad = dot_nt(v_ref[0, where, :], upstream)
            score_low = (probs * (prob_grad - delta)).astype(BF16)
            dk_part = jnp.dot(score_low, queries, preferred_element_type=F32)
            dv_part = jnp.dot(probs.astype(BF16), upstream, preferred_element_type=F32)
            if first:
                dk_sum[where, :] = dk_part
                dv_sum[where, :] = dv_part
            else:
                dk_sum[where, :] += dk_part
                dv_sum[where, :] += dv_part
            return dot_tn(keys, score_low)

        dq = part(here, True)
        if i:
            dq = dq + part(pl.ds(0, i * rows), False)
        dq_ref[0, here, :] = dq.T.astype(BF16)
    dk_ref[0] = dk_sum[...].astype(BF16)
    dv_ref[0] = dv_sum[...].astype(BF16)


def head_block(length):
    return pl.BlockSpec((1, length, HD), lambda h: (h, 0, 0))


def row_block(length):
    return pl.BlockSpec((1, 1, length), lambda h: (h, 0, 0))


def attend_forward(queries, keys, values):
    heads, length, _ = queries.shape
    pairs = heads * length * length // 2
    return pl.pallas_call(
        forward_kernel,
        grid=(heads,),
        in_specs=[head_block(length)] * 3,
        out_specs=[head_block(length), row_block(length)],
        out_shape=[
            jax.ShapeDtypeStruct((heads, length, HD), BF16),
            jax.ShapeDtypeStruct((heads, 1, length), F32),
        ],
        compiler_params=pltpu.CompilerParams(vmem_limit_bytes=VMEM_LIMIT),
        cost_estimate=pl.CostEstimate(
            flops=16 * pairs * HD, bytes_accessed=8 * heads * length * HD, transcendentals=pairs
        ),
    )(queries, keys, values)


def attend_backward(queries, keys, values, attended, log_total, upstream):
    heads, length, _ = queries.shape
    pairs = heads * length * length // 2
    return pl.pallas_call(
        backward_kernel,
        grid=(heads,),
        in_specs=[head_block(length)] * 4 + [row_block(length), head_block(length)],
        out_specs=[head_block(length)] * 3,
        out_shape=[jax.ShapeDtypeStruct((heads, length, HD), BF16)] * 3,
        scratch_shapes=[pltpu.VMEM((length, HD), F32)] * 2,
        compiler_params=pltpu.CompilerParams(vmem_limit_bytes=VMEM_LIMIT),
        cost_estimate=pl.CostEstimate(
            flops=40 * pairs * HD, bytes_accessed=16 * heads * length * HD, transcendentals=pairs
        ),
    )(queries, keys, values, attended, log_total, upstream)


def to_heads(arrays):
    seqs, block, width = arrays[0].shape
    members = lax.axis_size("ctx")
    group = members // seqs
    held = -(-H // group)
    count = len(arrays)
    stacked = jnp.stack(arrays)
    padded = group * held * HD
    if padded > width:
        stacked = jnp.pad(stacked, ((0, 0), (0, 0), (0, 0), (0, padded - width)))
    stacked = stacked.reshape(count, seqs, block, group, held * HD)
    stacked = stacked.transpose(1, 3, 2, 0, 4).reshape(members, block, count * held * HD)
    moved = lax.all_to_all(stacked, "ctx", 0, 0)
    moved = moved.reshape(members * block, count, held, HD).transpose(1, 2, 0, 3)
    return [moved[i] for i in range(count)]


def to_tokens(arrays, seqs, block, width):
    members = lax.axis_size("ctx")
    group = members // seqs
    held = arrays[0].shape[0]
    count = len(arrays)
    stacked = jnp.stack(arrays).transpose(2, 0, 1, 3).reshape(members, block, count * held * HD)
    moved = lax.all_to_all(stacked, "ctx", 0, 0)
    moved = moved.reshape(seqs, group, block, count, held * HD).transpose(3, 0, 2, 1, 4)
    moved = moved.reshape(count, seqs * block, group * held * HD)[:, :, :width]
    return [moved[i] for i in range(count)]


def across(value, axis, bit):
    size = lax.axis_size(axis)
    return lax.ppermute(value, axis, [(i, i ^ bit) for i in range(size)])


def halves(pair, axis, bit, dim):
    side = (lax.axis_index(axis) // bit) % 2
    kept = lax.dynamic_index_in_dim(pair, side, dim, keepdims=False)
    given = lax.dynamic_index_in_dim(pair, 1 - side, dim, keepdims=False)
    return (kept.astype(F32) + across(given, axis, bit).astype(F32)).astype(BF16)


def doubled(part, axis, bit):
    side = (lax.axis_index(axis) // bit) % 2
    other = across(part, axis, bit)
    low = jnp.where(side == 0, part, other)
    high = jnp.where(side == 0, other, part)
    return jnp.concatenate([low, high], axis=0)


def bits_of(axis, first):
    bits = []
    while first < lax.axis_size(axis):
        bits.append((axis, first))
        first *= 2
    return bits


def sum_shares(grad):
    width = grad.shape[1]
    stages = bits_of("dp", 1) + bits_of("ctx", 2)
    part = halves(grad.astype(BF16).reshape(2, 2, -1, width), "ctx", 1, 1)
    part = halves(part, "fsdp", 1, 0)
    for axis, bit in stages:
        part = halves(part.reshape(2, -1, width), axis, bit, 0)
    for axis, bit in reversed(stages):
        part = doubled(part, axis, bit)
    return doubled(part, "ctx", 1).astype(F32)


def gather_weight(shard):
    rows, width = shard.shape
    side = lax.axis_index("ctx") % 2
    mine = lax.dynamic_index_in_dim(shard.reshape(2, rows // 2, width), side, 0, keepdims=False)
    theirs = doubled(across(mine, "fsdp", 1), "ctx", 1)
    place = lax.axis_index("fsdp")
    low = jnp.where(place == 0, shard, theirs)
    high = jnp.where(place == 0, theirs, shard)
    return jnp.concatenate([low, high], axis=0)


def per_device(
    inputs,
    w_qkv,
    w_out,
    w_up,
    w_down,
    ln1_gain,
    ln1_bias,
    q_bias,
    v_bias,
    out_bias,
    ln2_gain,
    ln2_bias,
    up_bias,
    down_bias,
    cotangent,
):
    qkv_full = gather_weight(w_qkv)
    out_full = lax.all_gather(w_out, "fsdp", axis=0, tiled=True)
    up_full = lax.all_gather(w_up, "fsdp", axis=0, tiled=True)
    down_full = lax.all_gather(w_down, "fsdp", axis=0, tiled=True)
    short = [
        ln1_gain,
        ln1_bias,
        q_bias,
        v_bias,
        out_bias,
        ln2_gain,
        ln2_bias,
        down_bias,
    ]
    piece = ln1_gain.shape[0]
    packed = jnp.concatenate(short + [up_bias]).reshape(1, -1)
    packed = lax.all_gather(packed, "fsdp", axis=0, tiled=True)
    (
        gain_one,
        shift_one,
        query_shift,
        value_shift,
        branch_shift,
        gain_two,
        shift_two,
        final_shift,
    ) = [packed[:, i * piece : (i + 1) * piece].reshape(-1) for i in range(len(short))]
    hidden_shift = packed[:, len(short) * piece :].reshape(-1)
    seqs, block, width = inputs.shape
    tokens = seqs * block
    scale = HD ** (-0.5)
    flat_in = inputs.reshape(tokens, width).astype(jnp.float32)
    normed1, norm1_pull = jax.vjp(
        layer_norm, flat_in, gain_one.astype(jnp.float32), shift_one.astype(jnp.float32)
    )
    normed1_low = normed1.astype(jnp.bfloat16)
    projected = jnp.dot(normed1_low, qkv_full, preferred_element_type=jnp.float32)
    queries = (
        ((projected[:, :width] + query_shift.astype(jnp.float32)) * scale)
        .astype(jnp.bfloat16)
        .reshape(seqs, block, width)
    )
    keys = projected[:, width : 2 * width].astype(jnp.bfloat16).reshape(seqs, block, width)
    values = (
        (projected[:, 2 * width :] + value_shift.astype(jnp.float32))
        .astype(jnp.bfloat16)
        .reshape(seqs, block, width)
    )
    heads_q, heads_k, heads_v = to_heads([queries, keys, values])
    heads_o, log_total = attend_forward(heads_q, heads_k, heads_v)
    (attended_low,) = to_tokens([heads_o], seqs, block, width)
    middle = (
        flat_in
        + jnp.dot(attended_low, out_full, preferred_element_type=jnp.float32)
        + branch_shift.astype(jnp.float32)
    )
    normed2, norm2_pull = jax.vjp(
        layer_norm, middle, gain_two.astype(jnp.float32), shift_two.astype(jnp.float32)
    )
    normed2_low = normed2.astype(jnp.bfloat16)
    hidden = jnp.dot(
        normed2_low, up_full, preferred_element_type=jnp.float32
    ) + hidden_shift.astype(jnp.float32)
    activated, gelu_pull = jax.vjp(exact_gelu, hidden)
    activated_low = activated.astype(jnp.bfloat16)
    output = (
        middle
        + jnp.dot(activated_low, down_full, preferred_element_type=jnp.float32)
        + final_shift.astype(jnp.float32)
    )
    result = output.astype(jnp.bfloat16).reshape(seqs, block, width)
    upstream_low = cotangent.reshape(tokens, width)
    upstream = upstream_low.astype(jnp.float32)
    down_grad = jnp.einsum(
        "rf,rd->fd", activated_low, upstream_low, preferred_element_type=jnp.float32
    )
    final_shift_grad = jnp.sum(upstream, axis=0)
    activated_grad = jnp.einsum(
        "rd,fd->rf", upstream_low, down_full, preferred_element_type=jnp.float32
    )
    hidden_low = gelu_pull(activated_grad)[0].astype(jnp.bfloat16)
    up_grad = jnp.einsum("rd,rf->df", normed2_low, hidden_low, preferred_element_type=jnp.float32)
    hidden_shift_grad = jnp.sum(hidden_low.astype(jnp.float32), axis=0)
    normed2_grad = jnp.einsum("rf,df->rd", hidden_low, up_full, preferred_element_type=jnp.float32)
    middle_part, gain_two_grad, shift_two_grad = norm2_pull(normed2_grad)
    middle_grad = upstream + middle_part
    branch_low = middle_grad.astype(jnp.bfloat16)
    branch_shift_grad = jnp.sum(branch_low.astype(jnp.float32), axis=0)
    out_grad = jnp.einsum("rd,re->de", attended_low, branch_low, preferred_element_type=jnp.float32)
    attended_grad = (
        jnp.einsum("re,de->rd", branch_low, out_full, preferred_element_type=jnp.float32)
        .astype(jnp.bfloat16)
        .reshape(seqs, block, width)
    )
    share_down = sum_shares(down_grad)
    share_up = sum_shares(up_grad)
    share_out = sum_shares(out_grad)
    (heads_up,) = to_heads([attended_grad])
    query_acc, key_acc, value_acc = to_tokens(
        attend_backward(heads_q, heads_k, heads_v, heads_o, log_total, heads_up),
        seqs,
        block,
        width,
    )
    query_pre = (query_acc.astype(F32) * scale).astype(BF16)
    key_low, value_low = key_acc, value_acc
    stacked = jnp.concatenate([query_pre, key_low, value_low], axis=1)
    qkv_grad = jnp.einsum("rd,rf->df", normed1_low, stacked, preferred_element_type=jnp.float32)
    query_shift_grad = jnp.sum(query_pre.astype(jnp.float32), axis=0)
    value_shift_grad = jnp.sum(value_low.astype(jnp.float32), axis=0)
    normed1_grad = jnp.einsum("rf,df->rd", stacked, qkv_full, preferred_element_type=jnp.float32)
    input_part, gain_one_grad, shift_one_grad = norm1_pull(normed1_grad)
    input_grad = (middle_grad + input_part).astype(jnp.bfloat16).reshape(seqs, block, width)
    share_qkv = sum_shares(qkv_grad)
    shards = lax.axis_size("fsdp")
    row_grads = [
        gain_one_grad,
        shift_one_grad,
        query_shift_grad,
        value_shift_grad,
        branch_shift_grad,
        gain_two_grad,
        shift_two_grad,
        final_shift_grad,
        hidden_shift_grad,
    ]
    rows = jnp.concatenate([grad.reshape(shards, -1) for grad in row_grads], axis=1)
    rows = lax.psum(rows, ("dp", "ctx", "fsdp"))
    mine = lax.dynamic_index_in_dim(rows, lax.axis_index("fsdp"), 0, keepdims=False)
    parts = [mine[i * piece : (i + 1) * piece] for i in range(8)]
    return (
        result,
        input_grad,
        share_qkv,
        share_out,
        share_up,
        share_down,
        *parts[:7],
        mine[8 * piece :],
        parts[7],
    )


def solution(mesh):
    return jax.shard_map(
        per_device,
        mesh=mesh,
        in_specs=(
            P(("dp", "fsdp"), "ctx", None),
            P("fsdp", None),
            P("fsdp", None),
            P("fsdp", None),
            P("fsdp", None),
            P("fsdp"),
            P("fsdp"),
            P("fsdp"),
            P("fsdp"),
            P("fsdp"),
            P("fsdp"),
            P("fsdp"),
            P("fsdp"),
            P("fsdp"),
            P(("dp", "fsdp"), "ctx", None),
        ),
        out_specs=(
            P(("dp", "fsdp"), "ctx", None),
            P(("dp", "fsdp"), "ctx", None),
            P("fsdp", None),
            P("fsdp", None),
            P("fsdp", None),
            P("fsdp", None),
            P("fsdp"),
            P("fsdp"),
            P("fsdp"),
            P("fsdp"),
            P("fsdp"),
            P("fsdp"),
            P("fsdp"),
            P("fsdp"),
            P("fsdp"),
        ),
        check_vma=False,
    )
```

time: 1280 us -> 592 us (0.46)
  blocking collectives: 338 us -> 48.3 us
  waiting for transfers between devices: 478 us -> 212 us
  matrix products: 188 us -> 59.9 us
  other arithmetic: 116 us -> 53.2 us
  Pallas kernels: 0 us -> 42 us
  starting transfers between devices: 65.5 us -> 78.7 us
    psum x1, blocking collectives: 299 us -> 43.9 us  [per_device(): rows = lax.psum(rows, ('dp', 'ctx', 'fsdp'))]
    all_gather x6 -> x3, waiting for transfers between devices: 201 us -> 0.02 us  [the longest x1 0.02 us: per_device(): up_full = lax.all_gather(w_up, 'fsdp', axis=0, tiled=True)]
    reduce_scatter x4 -> x0, waiting for transfers between devices: 124 us -> none  [the longest x1 62.9 us: per_device(): lax.psum_scatter(down_grad.astype(jnp.bfloat16), 'fsdp', scatter_dimensio...]
    dot_general x48 -> x0, matrix products: 121 us -> none  [the longest x4 26.1 us: one_part(): jnp.einsum('sqhe,skhe->sqhk', query_heads, key_part, preferred_element_ty...]
    all_to_all x0 -> x4, waiting for transfers between devices: none -> 72.2 us  [the longest x2 53.1 us: to_heads(): moved = lax.all_to_all(stacked, 'ctx', 0, 0)]
    while x136 -> x0, local copies, waits for them, and re-layouts: 43.9 us -> none
    convert_element_type x46 -> x25, other arithmetic: 66.7 us -> 22.8 us  [the longest x20 14.1 us: halves(): (kept.astype(F32) + across(given, axis, bit).astype(F32)).astype(BF16)]
    pallas_call x0 -> x2, Pallas kernels: none -> 42 us  [the longest x1 23.8 us: attend_backward(): pl.pallas_call(backward_kernel, grid=(heads,), in_specs=[head_block(lengt...]
  transfers between devices with their start and end apart: 42 -> 45, of which waited for: 30 -> 18; matrix products, arithmetic and copies ran while one was open for 25% -> 26% of each run, Pallas kernels for 0% -> 7%
where the time goes in v1:
time: 592 us; the launch traced here: 588 us
  waiting for transfers between devices  212 us (36%)
  starting transfers between devices  78.7 us (13%)
  local copies, waits for them, and re-layouts  78.3 us (13%)
  matrix products  59.9 us (10%)
  other arithmetic  53.2 us (9%)
  blocking collectives  48.3 us (8%)
  Pallas kernels  42 us (7%)
  between operations  15.9 us (3%)
    ppermute x38, waiting for transfers between devices, across(): return lax.ppermute(value, axis, [(i, i ^ bit) for i in range(size)])  138 us
    ppermute x38, starting transfers between devices, across(): return lax.ppermute(value, axis, [(i, i ^ bit) for i in range(size)])  56.1 us
    all_to_all x2, waiting for transfers between devices, to_heads(): moved = lax.all_to_all(stacked, 'ctx', 0, 0)  53.1 us
    psum x1, blocking collectives, per_device(): rows = lax.psum(rows, ('dp', 'ctx', 'fsdp'))  43.9 us
    pallas_call x1, Pallas kernels, attend_backward(): pl.pallas_call(backward_kernel, grid=(heads,), in_specs=[head_block(lengt...  23.8 us
    dot_general x1, matrix products, per_device(): jnp.einsum('rd,fd->rf', upstream_low, down_full, preferred_element_type=j...  19.1 us
    all_to_all x2, waiting for transfers between devices, to_tokens(): moved = lax.all_to_all(stacked, 'ctx', 0, 0)  19.1 us
    pallas_call x1, Pallas kernels, attend_forward(): pl.pallas_call(forward_kernel, grid=(heads,), in_specs=[head_block(length...  18.2 us
  transfers between devices with their start and end apart: 45, of which 18 were waited for; matrix products, arithmetic and copies ran while one was open for 26% of the time, Pallas kernels for 7%

profile of v1, /device:TPU:1, one launch (start us, length us, event | category | flops | bytes accessed | tf_op | source)
XLA Modules:
  0.0 588.0 jit_solution(15993691578037189450)
XLA Ops:
  11.7 28.1 %collective-permute-done = bf16[192,2304]{1,0:T(8,128)(2,1)S(1)} collective-permute-done((bf16[192,2304]{1,0:T(8,128)(2,1)S(1)}, bf16[192,2304]{1,0:T(8,128)(2,1)S(1)}, u32[]{:S(2)}, u32[]{:S(2)}) %collective-permute-start) | collective-permute-done | bytes 884768 | tf_op jit(solution)/shard_map/ppermute | solution.py:185
  45.8 4.5 all-gather.1
  65.5 4.0 maximum_bitcast_fusion.1
  71.4 5.5 all-to-all-start
  77.6 53.1 %all-to-all-done = bf16[8,256,576]{1,2,0:T(8,128)(2,1)S(1)} async-done(((bf16[8,256,576]{1,2,0:T(8,128)(2,1)}), bf16[8,256,576]{1,2,0:T(8,128)(2,1)S(1)}, u32[]{:S(2)}, u32[]{:S(2)}) %all-to-all-start) | async-done | bytes 2359328 | tf_op jit(solution)/shard_map/all_to_all | solution.py:166
  141.0 4.6 slice_bitcast_fusion
  145.6 18.2 %shard_map.262 = (bf16[3,2048,64]{2,1,0:T(8,128)(2,1)}, f32[3,1,2048]{2,1,0:T(1,128)}) custom-call(bf16[3,2048,64]{2,1,0:T(8,128)(2,1)} %get-tuple-element.51.q_ref, bf16[3,2048,64]{2,1,0:T(8,128)(2,1)} %get-tuple-element.50.k_ref, bf16[3,2048,64]{2,1,0:T(8,128)(2,1)} %get-tuple-element.49.v_ref), custom_call_target="tpu_custom_call" | custom-call | flops 6442450944 | bytes 3145728 | tf_op jit(solution)/shard_map/pallas_call | solution.py:121
  166.7 4.6 all-to-all-start.1
  172.4 19.1 %all-to-all-done.1 = bf16[8,256,192]{1,2,0:T(8,128)(2,1)S(1)} async-done(((bf16[8,256,192]{1,2,0:T(8,128)(2,1)}), bf16[8,256,192]{1,2,0:T(8,128)(2,1)S(1)}, u32[]{:S(2)}, u32[]{:S(2)}) %all-to-all-start.1) | async-done | bytes 786464 | tf_op jit(solution)/shard_map/all_to_all | solution.py:177
  196.1 7.2 %fusion.50 = f32[512,3072]{1,0:T(8,128)} fusion(bf16[768,3072]{1,0:T(8,128)(2,1)} %all-gather.8.cloned.1.call-done, f32[512,768]{1,0:T(8,128)S(1)} %get-tuple-element.104, f32[768]{0:T(1024)S(1)} %reshape.418, f32[768]{0:T(1024)S(1)} %reshape.417, f32[512]{0:T(512)S(1)} %fusion.44, f32[512]{0:T(512)S(1)} %broadcast_multiply_fusion), kind=kOutput, calls=%fused_computation.228 | convolution fusion | flops 2417885184 | bytes 12593152 | tf_op jit(solution)/shard_map/dot_general | solution.py:311
  203.3 19.1 %convert_reduce_fusion = (f32[3072]{0:T(1024)S(1)}, bf16[512,3072]{1,0:T(8,128)(2,1)S(1)}, f32[512,3072]{1,0:T(8,128)S(1)}) fusion(f32[512,3072]{1,0:T(8,128)} %fusion.50, f32[3072]{0:T(1024)S(1)} %reshape.419, bf16[512,768]{1,0:T(8,128)(2,1)S(1)} %bitcast.259, bf16[3072,768]{1,0:T(8,128)(2,1)} %all-gather.10.cloned.1.call-done), kind=kOutput, calls=%fused_computation.2 | convolution fusion | flops 2533880832 | bytes 21258240 | tf_op jit(solution)/shard_map/rd,fd->rf/dot_general | solution.py:328
  235.9 6.4 %convolution_convert_fusion.1 = bf16[768,3072]{1,0:T(8,128)(2,1)} fusion(bf16[512,3072]{1,0:T(8,128)(2,1)} %copy-done.53, f32[512,768]{1,0:T(8,128)S(1)} %copy-done.6, f32[768]{0:T(1024)S(1)} %reshape.418, f32[768]{0:T(1024)S(1)} %reshape.417, f32[512]{0:T(512)S(1)} %fusion.44, f32[512]{0:T(512)S(1)} %broadcast_multiply_fusion), kind=kOutput, calls=%fused_computation.19 | convolution fusion | flops 2420244480 | bytes 9447424 | tf_op jit(solution)/shard_map/rd,rf->df/dot_general | solution.py:332
  251.6 4.5 all-to-all-start.2
  262.7 8.2 %collective-permute-done.14 = bf16[48,768]{1,0:T(8,128)(2,1)S(1)} collective-permute-done((bf16[48,768]{1,0:T(8,128)(2,1)S(1)}, bf16[48,768]{1,0:T(8,128)(2,1)S(1)}, u32[]{:S(2)}, u32[]{:S(2)}) %collective-permute-start.14) | collective-permute-done | bytes 73760 | tf_op jit(solution)/shard_map/ppermute | solution.py:185
  270.9 4.1 collective-permute-start.15
  275.0 5.8 add_convert_fusion.2
  293.3 23.8 %shard_map.263 = (bf16[3,2048,64]{2,1,0:T(8,128)(2,1)}, bf16[3,2048,64]{2,1,0:T(8,128)(2,1)}, bf16[3,2048,64]{2,1,0:T(8,128)(2,1)}) custom-call(bf16[3,2048,64]{2,1,0:T(8,128)(2,1)} %get-tuple-element.51.q_ref, bf16[3,2048,64]{2,1,0:T(8,128)(2,1)} %get-tuple-element.50.k_ref, bf16[3,2048,64]{2,1,0:T(8,128)(2,1)} %get-tuple-element.49.v_ref, ...), custom_call_target="tpu_custom_call" | custom-call | flops 16106127360 | bytes 6291456 | tf_op jit(solution)/shard_map/pallas_call | solution.py:140
  327.4 6.0 %copy.60 = bf16[2048,3,3,64]{0,3,2,1:T(8,128)(2,1)} copy(bf16[2048,3,3,64]{3,0,2,1:T(8,128)(2,1)} %maximum_bitcast_fusion) | data formatting | bytes 4718592 | tf_op jit(solution)/shard_map/transpose | solution.py:176
  337.7 7.7 %all-to-all-start.3 = ((bf16[8,256,576]{1,2,0:T(8,128)(2,1)}), bf16[8,256,576]{1,2,0:T(8,128)(2,1)}, u32[]{:S(2)}, u32[]{:S(2)}) async-start(bf16[8,256,576]{1,2,0:T(8,128)(2,1)} %copy.61), calls=%async_computation.3 | async-start | bytes 4718592 | tf_op jit(solution)/shard_map/all_to_all | solution.py:177
  355.5 21.5 %collective-permute-done.30 = bf16[768,768]{1,0:T(8,128)(2,1)S(1)} collective-permute-done((bf16[768,768]{1,0:T(8,128)(2,1)S(1)}, bf16[768,768]{1,0:T(8,128)(2,1)S(1)}, u32[]{:S(2)}, u32[]{:S(2)}) %collective-permute-start.30) | collective-permute-done | bytes 1179680 | tf_op jit(solution)/shard_map/ppermute | solution.py:185
  380.9 10.4 %collective-permute-done.31 = bf16[384,768]{1,0:T(8,128)(2,1)S(1)} collective-permute-done((bf16[384,768]{1,0:T(8,128)(2,1)S(1)}, bf16[384,768]{1,0:T(8,128)(2,1)S(1)}, u32[]{:S(2)}, u32[]{:S(2)}) %collective-permute-start.31) | collective-permute-done | bytes 589856 | tf_op jit(solution)/shard_map/ppermute | solution.py:185
  395.7 13.1 %collective-permute-done.32 = bf16[192,768]{1,0:T(8,128)(2,1)S(1)} collective-permute-done((bf16[192,768]{1,0:T(8,128)(2,1)S(1)}, bf16[192,768]{1,0:T(8,128)(2,1)S(1)}, u32[]{:S(2)}, u32[]{:S(2)}) %collective-permute-start.32) | collective-permute-done | bytes 294944 | tf_op jit(solution)/shard_map/ppermute | solution.py:185
  411.5 9.5 %collective-permute-done.33 = bf16[96,768]{1,0:T(8,128)(2,1)S(1)} collective-permute-done((bf16[96,768]{1,0:T(8,128)(2,1)S(1)}, bf16[96,768]{1,0:T(8,128)(2,1)S(1)}, u32[]{:S(2)}, u32[]{:S(2)}) %collective-permute-start.33) | collective-permute-done | bytes 147488 | tf_op jit(solution)/shard_map/ppermute | solution.py:185
  426.4 4.1 collective-permute-done.34
  431.4 5.4 collective-permute-done.26
  454.3 6.4 %fusion.51 = (f32[768]{0:T(1024)S(1)}, f32[512]{0:T(512)S(1)}, f32[512,768]{1,0:T(8,128)}) fusion(f32[768]{0:T(1024)S(1)} %copy-done.34, f32[512]{0:T(512)S(1)} %bitcast.319, bf16[2,256,768]{2,1,0:T(8,128)(2,1)S(1)} %copy-done.1, bf16[512,2304]{0,1:T(8,128)(2,1)} %copy-done.32, bf16[384,2304]{1,0:T(8,128)(2,1)} %copy-done.21, bf16[384,2304]{1,0:T(8,128)(2,1)} %copy-done.20), kind=kOutput, calls=%fused_computation.229 | convolution fusion | flops 1821375232 | bytes 8267776 | tf_op jit(solution)/shard_map/rf,df->rd/dot_general | solution.py:361
  466.0 19.8 %collective-permute-done.3 = bf16[192,2304]{1,0:T(8,128)(2,1)S(1)} collective-permute-done((bf16[192,2304]{1,0:T(8,128)(2,1)S(1)}, bf16[192,2304]{1,0:T(8,128)(2,1)S(1)}, u32[]{:S(2)}, u32[]{:S(2)}) %collective-permute-start.3) | collective-permute-done | bytes 884768 | tf_op jit(solution)/shard_map/ppermute | solution.py:185
  489.0 43.9 %psum.7 = f32[2,4608]{1,0:T(2,128)S(1)} all-reduce(f32[2,4608]{1,0:T(2,128)S(1)} %constant_dynamic-update-slice_fusion.3), channel_id=1, replica_groups=mesh['dp'=2,'ctx'=8,'fsdp'=2] {'dp','ctx','fsdp'}, use_global_device_ids=true, to_apply=%region_17.18 | all-reduce | flops 9216 | bytes 73728 | tf_op jit(solution)/shard_map/psum | solution.py:378
  547.2 4.6 collective-permute-start.28
  553.8 5.1 collective-permute-start.37
  562.0 5.4 collective-permute-done.9
  567.7 5.1 collective-permute-start.10
  (369 shorter events, 183.2 us)
Async XLA Ops:
  7.2 186.1 %all-gather.6.cloned.1.call-start = ((), (), s32[]{:S(2)}) async-start(), calls=%async_computation.4 | async-start | bytes 1769472 | tf_op jit(solution)/shard_map/all_gather | solution.py:252
  7.9 188.2 %all-gather.8.cloned.1.call-start = ((), (), s32[]{:S(2)}) async-start(), calls=%async_computation.5 | async-start | bytes 7077888 | tf_op jit(solution)/shard_map/all_gather | solution.py:253
  9.3 30.4 %collective-permute-start = (bf16[192,2304]{1,0:T(8,128)(2,1)S(1)}, bf16[192,2304]{1,0:T(8,128)(2,1)S(1)}, u32[]{:S(2)}, u32[]{:S(2)}) collective-permute-start(bf16[192,2304]{1,0:T(8,128)(2,1)S(1)} %dynamic-slice_bitcast_fusion.6), channel_id=1, source_target_pairs={{0,1},{1,0},{2,3},{3,2},{4,5},{5,4},{6,7},{7,6},{8,9},{9,8},{10,11... | collective-permute-start | bytes 2654216 | tf_op jit(solution)/shard_map/ppermute | solution.py:185
  39.8 11.1 %collective-permute-start.1 = (bf16[192,2304]{1,0:T(8,128)(2,1)S(1)}, bf16[192,2304]{1,0:T(8,128)(2,1)S(1)}, u32[]{:S(2)}, u32[]{:S(2)}) collective-permute-start(bf16[192,2304]{1,0:T(8,128)(2,1)S(1)} %collective-permute-done), channel_id=1, source_target_pairs={{0,2},{2,0},{4,6},{6,4},{8,10},{10,8},{12,14},{14,12},{1,3},{3,1},... | collective-permute-start | bytes 2654216 | tf_op jit(solution)/shard_map/ppermute | solution.py:185
  71.4 59.3 %all-to-all-start = ((bf16[8,256,576]{1,2,0:T(8,128)(2,1)}), bf16[8,256,576]{1,2,0:T(8,128)(2,1)S(1)}, u32[]{:S(2)}, u32[]{:S(2)}) async-start(bf16[8,256,576]{1,2,0:T(8,128)(2,1)} %bitcast.257), calls=%async_computation | async-start | bytes 4718592 | tf_op jit(solution)/shard_map/all_to_all | solution.py:166
  76.9 126.5 %all-gather.10.cloned.1.call-start = ((), (), s32[]{:S(2)}) async-start(), calls=%async_computation.6 | async-start | bytes 7077888 | tf_op jit(solution)/shard_map/all_gather | solution.py:254
  166.7 24.7 %all-to-all-start.1 = ((bf16[8,256,192]{1,2,0:T(8,128)(2,1)}), bf16[8,256,192]{1,2,0:T(8,128)(2,1)S(1)}, u32[]{:S(2)}, u32[]{:S(2)}) async-start(bf16[8,256,192]{1,2,0:T(8,128)(2,1)} %copy.54), calls=%async_computation.1 | async-start | bytes 1572864 | tf_op jit(solution)/shard_map/all_to_all | solution.py:177
  244.0 12.1 %collective-permute-start.13 = (bf16[96,768]{1,0:T(8,128)(2,1)}, bf16[96,768]{1,0:T(8,128)(2,1)}, u32[]{:S(2)}, u32[]{:S(2)}) collective-permute-start(bf16[96,768]{1,0:T(8,128)(2,1)} %dynamic-slice_bitcast_fusion.17), channel_id=1, source_target_pairs={{0,16},{16,0},{1,17},{17,1},{2,18},{18,2},{3,19},{19,3},{4,20},{20... | collective-permute-start | bytes 442376 | tf_op jit(solution)/shard_map/ppermute | solution.py:185
  251.6 37.4 %all-to-all-start.2 = ((bf16[8,256,192]{1,2,0:T(8,128)(2,1)}), bf16[8,256,192]{1,2,0:T(8,128)(2,1)S(1)}, u32[]{:S(2)}, u32[]{:S(2)}) async-start(bf16[8,256,192]{1,2,0:T(8,128)(2,1)} %bitcast.277), calls=%async_computation.2 | async-start | bytes 1572864 | tf_op jit(solution)/shard_map/all_to_all | solution.py:166
  257.1 13.7 %collective-permute-start.14 = (bf16[48,768]{1,0:T(8,128)(2,1)S(1)}, bf16[48,768]{1,0:T(8,128)(2,1)S(1)}, u32[]{:S(2)}, u32[]{:S(2)}) collective-permute-start(bf16[48,768]{1,0:T(8,128)(2,1)S(1)} %dynamic-slice_bitcast_fusion.19), channel_id=1, source_target_pairs={{0,4},{2,6},{4,0},{6,2},{8,12},{10,14},{12,8},{14,10},{1,5},{3,7},... | collective-permute-start | bytes 221192 | tf_op jit(solution)/shard_map/ppermute | solution.py:185
  262.0 55.1 %collective-permute-start.20 = (bf16[2,192,3072]{2,1,0:T(8,128)(2,1)}, bf16[2,192,3072]{2,1,0:T(8,128)(2,1)}, u32[]{:S(2)}, u32[]{:S(2)}) collective-permute-start(bf16[2,192,3072]{2,1,0:T(8,128)(2,1)} %dynamic-slice_bitcast_fusion.1), channel_id=1, source_target_pairs={{0,2},{2,0},{4,6},{6,4},{8,10},{10,8},{12,14},{14,12},{1,3},{3,1},... | collective-permute-start | bytes 7077896 | tf_op jit(solution)/shard_map/ppermute | solution.py:185
  286.8 59.8 %collective-permute-start.29 = (bf16[2,768,768]{2,1,0:T(8,128)(2,1)}, bf16[2,768,768]{2,1,0:T(8,128)(2,1)}, u32[]{:S(2)}, u32[]{:S(2)}) collective-permute-start(bf16[2,768,768]{2,1,0:T(8,128)(2,1)} %dynamic-slice_bitcast_fusion), channel_id=1, source_target_pairs={{0,2},{2,0},{4,6},{6,4},{8,10},{10,8},{12,14},{14,12},{1,3},{3,1},... | collective-permute-start | bytes 7077896 | tf_op jit(solution)/shard_map/ppermute | solution.py:185
  288.7 56.7 %collective-permute-start.18 = (bf16[96,768]{1,0:T(8,128)(2,1)S(1)}, bf16[96,768]{1,0:T(8,128)(2,1)}, u32[]{:S(2)}, u32[]{:S(2)}) collective-permute-start(bf16[96,768]{1,0:T(8,128)(2,1)S(1)} %pad_maximum_fusion.14), channel_id=1, source_target_pairs={{0,16},{16,0},{1,17},{17,1},{2,18},{18,2},{3,19},{19,3},{4,20},{20... | collective-permute-start | bytes 442376 | tf_op jit(solution)/shard_map/ppermute | solution.py:185
  323.1 27.0 %collective-permute-start.21 = (bf16[192,3072]{1,0:T(8,128)(2,1)}, bf16[192,3072]{1,0:T(8,128)(2,1)}, u32[]{:S(2)}, u32[]{:S(2)}) collective-permute-start(bf16[192,3072]{1,0:T(8,128)(2,1)} %dynamic-slice_bitcast_fusion.4), channel_id=1, source_target_pairs={{0,1},{1,0},{2,3},{3,2},{4,5},{5,4},{6,7},{7,6},{8,9},{9,8},{10,11... | collective-permute-start | bytes 3538952 | tf_op jit(solution)/shard_map/ppermute | solution.py:185
  337.7 100.0 %all-to-all-start.3 = ((bf16[8,256,576]{1,2,0:T(8,128)(2,1)}), bf16[8,256,576]{1,2,0:T(8,128)(2,1)}, u32[]{:S(2)}, u32[]{:S(2)}) async-start(bf16[8,256,576]{1,2,0:T(8,128)(2,1)} %copy.61), calls=%async_computation.3 | async-start | bytes 4718592 | tf_op jit(solution)/shard_map/all_to_all | solution.py:177
  349.7 27.4 %collective-permute-start.30 = (bf16[768,768]{1,0:T(8,128)(2,1)S(1)}, bf16[768,768]{1,0:T(8,128)(2,1)S(1)}, u32[]{:S(2)}, u32[]{:S(2)}) collective-permute-start(bf16[768,768]{1,0:T(8,128)(2,1)S(1)} %dynamic-slice_bitcast_fusion.3), channel_id=1, source_target_pairs={{0,1},{1,0},{2,3},{3,2},{4,5},{5,4},{6,7},{7,6},{8,9},{9,8},{10,11... | collective-permute-start | bytes 3538952 | tf_op jit(solution)/shard_map/ppermute | solution.py:185
  353.0 25.8 %collective-permute-start.22 = (bf16[96,3072]{1,0:T(8,128)(2,1)S(1)}, bf16[96,3072]{1,0:T(8,128)(2,1)S(1)}, u32[]{:S(2)}, u32[]{:S(2)}) collective-permute-start(bf16[96,3072]{1,0:T(8,128)(2,1)S(1)} %dynamic-slice_bitcast_fusion.8), channel_id=1, source_target_pairs={{0,16},{16,0},{1,17},{17,1},{2,18},{18,2},{3,19},{19,3},{4,20},{20... | collective-permute-start | bytes 1769480 | tf_op jit(solution)/shard_map/ppermute | solution.py:185
  377.4 13.8 %collective-permute-start.31 = (bf16[384,768]{1,0:T(8,128)(2,1)S(1)}, bf16[384,768]{1,0:T(8,128)(2,1)S(1)}, u32[]{:S(2)}, u32[]{:S(2)}) collective-permute-start(bf16[384,768]{1,0:T(8,128)(2,1)S(1)} %dynamic-slice_bitcast_fusion.7), channel_id=1, source_target_pairs={{0,16},{16,0},{1,17},{17,1},{2,18},{18,2},{3,19},{19,3},{4,20},{20... | collective-permute-start | bytes 1769480 | tf_op jit(solution)/shard_map/ppermute | solution.py:185
  379.0 14.6 %collective-permute-start.23 = (bf16[48,3072]{1,0:T(8,128)(2,1)S(1)}, bf16[48,3072]{1,0:T(8,128)(2,1)S(1)}, u32[]{:S(2)}, u32[]{:S(2)}) collective-permute-start(bf16[48,3072]{1,0:T(8,128)(2,1)S(1)} %dynamic-slice_bitcast_fusion.12), channel_id=1, source_target_pairs={{0,4},{2,6},{4,0},{6,2},{8,12},{10,14},{12,8},{14,10},{1,5},{3,7},... | collective-permute-start | bytes 884744 | tf_op jit(solution)/shard_map/ppermute | solution.py:185
  391.4 17.4 %collective-permute-start.32 = (bf16[192,768]{1,0:T(8,128)(2,1)S(1)}, bf16[192,768]{1,0:T(8,128)(2,1)S(1)}, u32[]{:S(2)}, u32[]{:S(2)}) collective-permute-start(bf16[192,768]{1,0:T(8,128)(2,1)S(1)} %dynamic-slice_bitcast_fusion.11), channel_id=1, source_target_pairs={{0,4},{2,6},{4,0},{6,2},{8,12},{10,14},{12,8},{14,10},{1,5},{3,7},... | collective-permute-start | bytes 884744 | tf_op jit(solution)/shard_map/ppermute | solution.py:185
  393.7 15.4 %collective-permute-start.24 = (bf16[24,3072]{1,0:T(8,128)(2,1)S(1)}, bf16[24,3072]{1,0:T(8,128)(2,1)S(1)}, u32[]{:S(2)}, u32[]{:S(2)}) collective-permute-start(bf16[24,3072]{1,0:T(8,128)(2,1)S(1)} %dynamic-slice_bitcast_fusion.16), channel_id=1, source_target_pairs={{0,8},{2,10},{4,12},{6,14},{8,0},{10,2},{12,4},{14,6},{1,9},{3,11}... | collective-permute-start | bytes 442376 | tf_op jit(solution)/shard_map/ppermute | solution.py:185
  409.0 12.0 %collective-permute-start.33 = (bf16[96,768]{1,0:T(8,128)(2,1)S(1)}, bf16[96,768]{1,0:T(8,128)(2,1)S(1)}, u32[]{:S(2)}, u32[]{:S(2)}) collective-permute-start(bf16[96,768]{1,0:T(8,128)(2,1)S(1)} %dynamic-slice_bitcast_fusion.15), channel_id=1, source_target_pairs={{0,8},{2,10},{4,12},{6,14},{8,0},{10,2},{12,4},{14,6},{1,9},{3,11}... | collective-permute-start | bytes 442376 | tf_op jit(solution)/shard_map/ppermute | solution.py:185
  409.1 15.1 %collective-permute-start.25 = (bf16[24,3072]{1,0:T(8,128)(2,1)S(1)}, bf16[24,3072]{1,0:T(8,128)(2,1)S(1)}, u32[]{:S(2)}, u32[]{:S(2)}) collective-permute-start(bf16[24,3072]{1,0:T(8,128)(2,1)S(1)} %fusion.39), channel_id=1, source_target_pairs={{0,8},{2,10},{4,12},{6,14},{8,0},{10,2},{12,4},{14,6},{1,9},{3,11}... | collective-permute-start | bytes 442376 | tf_op jit(solution)/shard_map/ppermute | solution.py:185
  424.2 12.6 %collective-permute-start.26 = (bf16[48,3072]{1,0:T(8,128)(2,1)S(1)}, bf16[48,3072]{1,0:T(8,128)(2,1)S(1)}, u32[]{:S(2)}, u32[]{:S(2)}) collective-permute-start(bf16[48,3072]{1,0:T(8,128)(2,1)S(1)} %pad_maximum_fusion.11), channel_id=1, source_target_pairs={{0,4},{2,6},{4,0},{6,2},{8,12},{10,14},{12,8},{14,10},{1,5},{3,7},... | collective-permute-start | bytes 884744 | tf_op jit(solution)/shard_map/ppermute | solution.py:185
  431.4 19.8 %collective-permute-start.35 = (bf16[192,768]{1,0:T(8,128)(2,1)}, bf16[192,768]{1,0:T(8,128)(2,1)}, u32[]{:S(2)}, u32[]{:S(2)}) collective-permute-start(bf16[192,768]{1,0:T(8,128)(2,1)} %pad_maximum_fusion.12), channel_id=1, source_target_pairs={{0,4},{2,6},{4,0},{6,2},{8,12},{10,14},{12,8},{14,10},{1,5},{3,7},... | collective-permute-start | bytes 884744 | tf_op jit(solution)/shard_map/ppermute | solution.py:185
  448.5 14.4 %collective-permute-start.2 = (bf16[2,192,2304]{2,1,0:T(8,128)(2,1)}, bf16[2,192,2304]{2,1,0:T(8,128)(2,1)}, u32[]{:S(2)}, u32[]{:S(2)}) collective-permute-start(bf16[2,192,2304]{2,1,0:T(8,128)(2,1)} %dynamic-slice_bitcast_fusion.2), channel_id=1, source_target_pairs={{0,2},{2,0},{4,6},{6,4},{8,10},{10,8},{12,14},{14,12},{1,3},{3,1},... | collective-permute-start | bytes 5308424 | tf_op jit(solution)/shard_map/ppermute | solution.py:185
  450.0 91.7 %collective-permute-start.27 = (bf16[96,3072]{1,0:T(8,128)(2,1)}, bf16[96,3072]{1,0:T(8,128)(2,1)}, u32[]{:S(2)}, u32[]{:S(2)}) collective-permute-start(bf16[96,3072]{1,0:T(8,128)(2,1)} %pad_maximum_fusion.7), channel_id=1, source_target_pairs={{0,16},{16,0},{1,17},{17,1},{2,18},{18,2},{3,19},{19,3},{4,20},{20... | collective-permute-start | bytes 1769480 | tf_op jit(solution)/shard_map/ppermute | solution.py:185
  453.9 98.5 %collective-permute-start.36 = (bf16[384,768]{1,0:T(8,128)(2,1)}, bf16[384,768]{1,0:T(8,128)(2,1)}, u32[]{:S(2)}, u32[]{:S(2)}) collective-permute-start(bf16[384,768]{1,0:T(8,128)(2,1)} %pad_maximum_fusion.8), channel_id=1, source_target_pairs={{0,16},{16,0},{1,17},{17,1},{2,18},{18,2},{3,19},{19,3},{4,20},{20... | collective-permute-start | bytes 1769480 | tf_op jit(solution)/shard_map/ppermute | solution.py:185
  465.4 20.4 %collective-permute-start.3 = (bf16[192,2304]{1,0:T(8,128)(2,1)S(1)}, bf16[192,2304]{1,0:T(8,128)(2,1)S(1)}, u32[]{:S(2)}, u32[]{:S(2)}) collective-permute-start(bf16[192,2304]{1,0:T(8,128)(2,1)S(1)} %dynamic-slice_bitcast_fusion.5), channel_id=1, source_target_pairs={{0,1},{1,0},{2,3},{3,2},{4,5},{5,4},{6,7},{7,6},{8,9},{9,8},{10,11... | collective-permute-start | bytes 2654216 | tf_op jit(solution)/shard_map/ppermute | solution.py:185
  487.7 46.6 %collective-permute-start.4 = (bf16[96,2304]{1,0:T(8,128)(2,1)}, bf16[96,2304]{1,0:T(8,128)(2,1)}, u32[]{:S(2)}, u32[]{:S(2)}) collective-permute-start(bf16[96,2304]{1,0:T(8,128)(2,1)} %dynamic-slice_bitcast_fusion.10), channel_id=1, source_target_pairs={{0,16},{16,0},{1,17},{17,1},{2,18},{18,2},{3,19},{19,3},{4,20},{20... | collective-permute-start | bytes 1327112 | tf_op jit(solution)/shard_map/ppermute | solution.py:185
  547.2 14.2 %collective-permute-start.28 = (bf16[192,3072]{1,0:T(8,128)(2,1)S(1)}, bf16[192,3072]{1,0:T(8,128)(2,1)S(1)}, u32[]{:S(2)}, u32[]{:S(2)}) collective-permute-start(bf16[192,3072]{1,0:T(8,128)(2,1)S(1)} %pad_maximum_fusion.4), channel_id=1, source_target_pairs={{0,2},{2,0},{4,6},{6,4},{8,10},{10,8},{12,14},{14,12},{1,3},{3,1},... | collective-permute-start | bytes 3538952 | tf_op jit(solution)/shard_map/ppermute | solution.py:185
  553.8 19.0 %collective-permute-start.37 = (bf16[768,768]{1,0:T(8,128)(2,1)S(1)}, bf16[768,768]{1,0:T(8,128)(2,1)S(1)}, u32[]{:S(2)}, u32[]{:S(2)}) collective-permute-start(bf16[768,768]{1,0:T(8,128)(2,1)S(1)} %pad_maximum_fusion.5), channel_id=1, source_target_pairs={{0,2},{2,0},{4,6},{6,4},{8,10},{10,8},{12,14},{14,12},{1,3},{3,1},... | collective-permute-start | bytes 3538952 | tf_op jit(solution)/shard_map/ppermute | solution.py:185
  (69 other events, 679.7 us)
Sparse Core Ops, SparseCore 0:
  9.6 34.9 all-gather.5
  46.1 63.8 all-gather.7
  111.5 62.6 all-gather.9

commit v2 on v1

--- a/solution.py
+++ b/solution.py
@@ -218,6 +218,16 @@
     for axis, bit in reversed(stages):
         part = doubled(part, axis, bit)
     return doubled(part, "ctx", 1).astype(F32)
+
+
+def sum_vectors(rows):
+    place = lax.axis_index("fsdp")
+    kept = lax.dynamic_index_in_dim(rows, place, 0, keepdims=True)
+    given = lax.dynamic_index_in_dim(rows, 1 - place, 0, keepdims=True)
+    part = kept + across(given, "fsdp", 1)
+    for axis, bit in bits_of("ctx", 1) + bits_of("dp", 1):
+        part = part + across(part, axis, bit)
+    return part[0]
 
 
 def gather_weight(shard):
@@ -263,8 +273,7 @@
         down_bias,
     ]
     piece = ln1_gain.shape[0]
-    packed = jnp.concatenate(short + [up_bias]).reshape(1, -1)
-    packed = lax.all_gather(packed, "fsdp", axis=0, tiled=True)
+    packed = doubled(jnp.concatenate(short + [up_bias]).reshape(1, -1), "fsdp", 1)
     (
         gain_one,
         shift_one,
@@ -375,8 +384,7 @@
         hidden_shift_grad,
     ]
     rows = jnp.concatenate([grad.reshape(shards, -1) for grad in row_grads], axis=1)
-    rows = lax.psum(rows, ("dp", "ctx", "fsdp"))
-    mine = lax.dynamic_index_in_dim(rows, lax.axis_index("fsdp"), 0, keepdims=False)
+    mine = sum_vectors(rows)
     parts = [mine[i * piece : (i + 1) * piece] for i in range(8)]
     return (
         result,

time: 592 us -> 550 us (0.929)
  blocking collectives: 48.3 us -> 0 us
  starting transfers between devices: 78.7 us -> 85.3 us
  waiting for transfers between devices: 212 us -> 218 us
    psum x1 -> x0, blocking collectives: 43.9 us -> none  [per_device(): rows = lax.psum(rows, ('dp', 'ctx', 'fsdp'))]
    ppermute x38 -> x44, starting transfers between devices: 56.1 us -> 62.6 us  [across(): return lax.ppermute(value, axis, [(i, i ^ bit) for i in range(size)])]
    ppermute x38 -> x44, waiting for transfers between devices: 138 us -> 144 us  [across(): return lax.ppermute(value, axis, [(i, i ^ bit) for i in range(size)])]
    unnamed x140 -> x132, local copies, waits for them, and re-layouts: 13.5 us -> 11.6 us
  transfers between devices with their start and end apart: 45 -> 51, of which waited for: 18 -> 23; matrix products, arithmetic and copies ran while one was open for 26% -> 27% of each run, Pallas kernels for 7% -> 8%
where the time goes in v2:
time: 550 us; the launch traced here: 540 us
  waiting for transfers between devices  218 us (40%)
  starting transfers between devices  85.3 us (16%)
  local copies, waits for them, and re-layouts  75.6 us (14%)
  matrix products  55.5 us (10%)
  other arithmetic  48.2 us (9%)
  Pallas kernels  42.2 us (8%)
  between operations  15.6 us (3%)
    ppermute x44, waiting for transfers between devices, across(): return lax.ppermute(value, axis, [(i, i ^ bit) for i in range(size)])  144 us
    ppermute x44, starting transfers between devices, across(): return lax.ppermute(value, axis, [(i, i ^ bit) for i in range(size)])  62.6 us
    all_to_all x2, waiting for transfers between devices, to_heads(): moved = lax.all_to_all(stacked, 'ctx', 0, 0)  53 us
    pallas_call x1, Pallas kernels, attend_backward(): pl.pallas_call(backward_kernel, grid=(heads,), in_specs=[head_block(lengt...  24 us
    all_to_all x2, waiting for transfers between devices, to_tokens(): moved = lax.all_to_all(stacked, 'ctx', 0, 0)  19.1 us
    dot_general x1, matrix products, per_device(): jnp.einsum('rd,fd->rf', upstream_low, down_full, preferred_element_type=j...  18.8 us
    pallas_call x1, Pallas kernels, attend_forward(): pl.pallas_call(forward_kernel, grid=(heads,), in_specs=[head_block(length...  18.2 us
    convert_element_type x20, other arithmetic, halves(): (kept.astype(F32) + across(given, axis, bit).astype(F32)).astype(BF16)  13 us
  transfers between devices with their start and end apart: 51, of which 23 were waited for; matrix products, arithmetic and copies ran while one was open for 27% of the time, Pallas kernels for 8%

profile of v2, /device:TPU:1, one launch (start us, length us, event | category | flops | bytes accessed | tf_op | source)
XLA Modules:
  0.0 540.2 jit_solution(13079187717213881279)
XLA Ops:
  14.0 25.6 %collective-permute-done.1 = bf16[192,2304]{1,0:T(8,128)(2,1)S(1)} collective-permute-done((bf16[192,2304]{1,0:T(8,128)(2,1)S(1)}, bf16[192,2304]{1,0:T(8,128)(2,1)S(1)}, u32[]{:S(2)}, u32[]{:S(2)}) %collective-permute-start.1) | collective-permute-done | bytes 884768 | tf_op jit(solution)/shard_map/ppermute | solution.py:185
  39.6 4.0 collective-permute-start.2
  59.2 4.0 maximum_bitcast_fusion.1
  65.0 5.6 %all-to-all-start = ((bf16[8,256,576]{1,2,0:T(8,128)(2,1)}), bf16[8,256,576]{1,2,0:T(8,128)(2,1)S(1)}, u32[]{:S(2)}, u32[]{:S(2)}) async-start(bf16[8,256,576]{1,2,0:T(8,128)(2,1)} %bitcast.254), calls=%async_computation | async-start | bytes 4718592 | tf_op jit(solution)/shard_map/all_to_all | solution.py:166
  71.4 53.0 %all-to-all-done = bf16[8,256,576]{1,2,0:T(8,128)(2,1)S(1)} async-done(((bf16[8,256,576]{1,2,0:T(8,128)(2,1)}), bf16[8,256,576]{1,2,0:T(8,128)(2,1)S(1)}, u32[]{:S(2)}, u32[]{:S(2)}) %all-to-all-start) | async-done | bytes 2359328 | tf_op jit(solution)/shard_map/all_to_all | solution.py:166
  127.2 3.7 reshape.376
  130.8 3.9 copy.52
  134.7 4.6 slice_bitcast_fusion
  139.3 18.2 %shard_map.262 = (bf16[3,2048,64]{2,1,0:T(8,128)(2,1)}, f32[3,1,2048]{2,1,0:T(1,128)}) custom-call(bf16[3,2048,64]{2,1,0:T(8,128)(2,1)} %get-tuple-element.51.q_ref, bf16[3,2048,64]{2,1,0:T(8,128)(2,1)} %get-tuple-element.50.k_ref, bf16[3,2048,64]{2,1,0:T(8,128)(2,1)} %get-tuple-element.49.v_ref), custom_call_target="tpu_custom_call" | custom-call | flops 6442450944 | bytes 3145728 | tf_op jit(solution)/shard_map/pallas_call | solution.py:121
  160.5 4.7 all-to-all-start.1
  166.2 19.1 %all-to-all-done.1 = bf16[8,256,192]{1,2,0:T(8,128)(2,1)S(1)} async-done(((bf16[8,256,192]{1,2,0:T(8,128)(2,1)}), bf16[8,256,192]{1,2,0:T(8,128)(2,1)S(1)}, u32[]{:S(2)}, u32[]{:S(2)}) %all-to-all-start.1) | async-done | bytes 786464 | tf_op jit(solution)/shard_map/all_to_all | solution.py:177
  190.0 7.2 %fusion.50 = f32[512,3072]{1,0:T(8,128)} fusion(bf16[768,3072]{1,0:T(8,128)(2,1)} %all-gather.6.cloned.1.call-done, f32[512,768]{1,0:T(8,128)S(1)} %get-tuple-element.106, f32[768]{0:T(1024)S(1)} %reshape.418, f32[768]{0:T(1024)S(1)} %reshape.417, f32[512]{0:T(512)S(1)} %fusion.44, f32[512]{0:T(512)S(1)} %broadcast_multiply_fusion), kind=kOutput, calls=%fused_computation.231 | convolution fusion | flops 2417885184 | bytes 12593152 | tf_op jit(solution)/shard_map/dot_general | solution.py:320
  197.2 18.8 %convert_reduce_fusion = (f32[3072]{0:T(1024)S(1)}, bf16[512,3072]{1,0:T(8,128)(2,1)S(1)}, f32[512,3072]{1,0:T(8,128)S(1)}) fusion(f32[512,3072]{1,0:T(8,128)} %fusion.50, f32[3072]{0:T(1024)S(1)} %reshape.419, bf16[512,768]{1,0:T(8,128)(2,1)S(1)} %bitcast.256, bf16[3072,768]{1,0:T(8,128)(2,1)} %all-gather.8.cloned.1.call-done), kind=kOutput, calls=%fused_computation.2 | convolution fusion | flops 2533880832 | bytes 21258240 | tf_op jit(solution)/shard_map/rd,fd->rf/dot_general | solution.py:337
  229.8 6.4 %convolution_convert_fusion.1 = bf16[768,3072]{1,0:T(8,128)(2,1)} fusion(bf16[512,3072]{1,0:T(8,128)(2,1)} %copy-done.50, f32[512,768]{1,0:T(8,128)S(1)} %copy-done.8, f32[768]{0:T(1024)S(1)} %reshape.418, f32[768]{0:T(1024)S(1)} %reshape.417, f32[512]{0:T(512)S(1)} %fusion.44, f32[512]{0:T(512)S(1)} %broadcast_multiply_fusion), kind=kOutput, calls=%fused_computation.19 | convolution fusion | flops 2420244480 | bytes 9447424 | tf_op jit(solution)/shard_map/rd,rf->df/dot_general | solution.py:341
  245.5 4.6 all-to-all-start.2
  256.6 8.2 %collective-permute-done.15 = bf16[48,768]{1,0:T(8,128)(2,1)S(1)} collective-permute-done((bf16[48,768]{1,0:T(8,128)(2,1)S(1)}, bf16[48,768]{1,0:T(8,128)(2,1)S(1)}, u32[]{:S(2)}, u32[]{:S(2)}) %collective-permute-start.15) | collective-permute-done | bytes 73760 | tf_op jit(solution)/shard_map/ppermute | solution.py:185
  264.9 4.1 collective-permute-start.16
  268.9 5.8 %add_convert_fusion.2 = bf16[512,768]{1,0:T(8,128)(2,1)} fusion(f32[512,768]{1,0:T(8,128)S(1)} %copy-done.9, bf16[512,3072]{1,0:T(8,128)(2,1)S(1)} %copy-done.13, bf16[3072,768]{1,0:T(8,128)(2,1)} %all-gather.8.cloned.1.call-done, f32[768]{0:T(1024)S(1)} %reshape.420), kind=kOutput, calls=%fused_computation.83 | convolution fusion | flops 2417098752 | bytes 10226688 | tf_op jit(solution)/shard_map/dot_general | solution.py:327
  287.2 24.0 %shard_map.263 = (bf16[3,2048,64]{2,1,0:T(8,128)(2,1)}, bf16[3,2048,64]{2,1,0:T(8,128)(2,1)}, bf16[3,2048,64]{2,1,0:T(8,128)(2,1)}) custom-call(bf16[3,2048,64]{2,1,0:T(8,128)(2,1)} %get-tuple-element.51.q_ref, bf16[3,2048,64]{2,1,0:T(8,128)(2,1)} %get-tuple-element.50.k_ref, bf16[3,2048,64]{2,1,0:T(8,128)(2,1)} %get-tuple-element.49.v_ref, ...), custom_call_target="tpu_custom_call" | custom-call | flops 16106127360 | bytes 6291456 | tf_op jit(solution)/shard_map/pallas_call | solution.py:140
  321.5 6.0 %copy.60 = bf16[2048,3,3,64]{0,3,2,1:T(8,128)(2,1)} copy(bf16[2048,3,3,64]{3,0,2,1:T(8,128)(2,1)} %maximum_bitcast_fusion) | data formatting | bytes 4718592 | tf_op jit(solution)/shard_map/transpose | solution.py:176
  331.9 7.6 %all-to-all-start.3 = ((bf16[8,256,576]{1,2,0:T(8,128)(2,1)}), bf16[8,256,576]{1,2,0:T(8,128)(2,1)}, u32[]{:S(2)}, u32[]{:S(2)}) async-start(bf16[8,256,576]{1,2,0:T(8,128)(2,1)} %copy.61), calls=%async_computation.3 | async-start | bytes 4718592 | tf_op jit(solution)/shard_map/all_to_all | solution.py:177
  349.6 21.5 %collective-permute-done.31 = bf16[768,768]{1,0:T(8,128)(2,1)S(1)} collective-permute-done((bf16[768,768]{1,0:T(8,128)(2,1)S(1)}, bf16[768,768]{1,0:T(8,128)(2,1)S(1)}, u32[]{:S(2)}, u32[]{:S(2)}) %collective-permute-start.31) | collective-permute-done | bytes 1179680 | tf_op jit(solution)/shard_map/ppermute | solution.py:185
  375.0 10.4 %collective-permute-done.32 = bf16[384,768]{1,0:T(8,128)(2,1)S(1)} collective-permute-done((bf16[384,768]{1,0:T(8,128)(2,1)S(1)}, bf16[384,768]{1,0:T(8,128)(2,1)S(1)}, u32[]{:S(2)}, u32[]{:S(2)}) %collective-permute-start.32) | collective-permute-done | bytes 589856 | tf_op jit(solution)/shard_map/ppermute | solution.py:185
  389.8 13.2 %collective-permute-done.33 = bf16[192,768]{1,0:T(8,128)(2,1)S(1)} collective-permute-done((bf16[192,768]{1,0:T(8,128)(2,1)S(1)}, bf16[192,768]{1,0:T(8,128)(2,1)S(1)}, u32[]{:S(2)}, u32[]{:S(2)}) %collective-permute-start.33) | collective-permute-done | bytes 294944 | tf_op jit(solution)/shard_map/ppermute | solution.py:185
  405.7 9.5 %collective-permute-done.34 = bf16[96,768]{1,0:T(8,128)(2,1)S(1)} collective-permute-done((bf16[96,768]{1,0:T(8,128)(2,1)S(1)}, bf16[96,768]{1,0:T(8,128)(2,1)S(1)}, u32[]{:S(2)}, u32[]{:S(2)}) %collective-permute-start.34) | collective-permute-done | bytes 147488 | tf_op jit(solution)/shard_map/ppermute | solution.py:185
  420.6 4.1 collective-permute-done.35
  425.6 5.4 %collective-permute-done.27 = bf16[48,3072]{1,0:T(8,128)(2,1)S(1)} collective-permute-done((bf16[48,3072]{1,0:T(8,128)(2,1)S(1)}, bf16[48,3072]{1,0:T(8,128)(2,1)S(1)}, u32[]{:S(2)}, u32[]{:S(2)}) %collective-permute-start.27) | collective-permute-done | bytes 294944 | tf_op jit(solution)/shard_map/ppermute | solution.py:185
  461.6 14.2 %collective-permute-done.4 = bf16[192,2304]{1,0:T(8,128)(2,1)S(1)} collective-permute-done((bf16[192,2304]{1,0:T(8,128)(2,1)S(1)}, bf16[192,2304]{1,0:T(8,128)(2,1)S(1)}, u32[]{:S(2)}, u32[]{:S(2)}) %collective-permute-start.4) | collective-permute-done | bytes 884768 | tf_op jit(solution)/shard_map/ppermute | solution.py:185
  479.4 7.7 %collective-permute-done.43 = f32[1,4608]{1,0:T(1,128)S(1)} collective-permute-done((f32[1,4608]{1,0:T(1,128)S(1)}, f32[1,4608]{1,0:T(1,128)S(1)}, u32[]{:S(2)}, u32[]{:S(2)}) %collective-permute-start.43) | collective-permute-done | bytes 18464 | tf_op jit(solution)/shard_map/ppermute | solution.py:185
  498.3 5.5 %collective-permute-start.29 = (bf16[192,3072]{1,0:T(8,128)(2,1)S(1)}, bf16[192,3072]{1,0:T(8,128)(2,1)S(1)}, u32[]{:S(2)}, u32[]{:S(2)}) collective-permute-start(bf16[192,3072]{1,0:T(8,128)(2,1)S(1)} %pad_maximum_fusion.4), channel_id=1, source_target_pairs={{0,2},{2,0},{4,6},{6,4},{8,10},{10,8},{12,14},{14,12},{1,3},{3,1},... | collective-permute-start | bytes 3538952 | tf_op jit(solution)/shard_map/ppermute | solution.py:185
  512.4 6.4 %collective-permute-done.10 = bf16[96,2304]{1,0:T(8,128)(2,1)S(1)} collective-permute-done((bf16[96,2304]{1,0:T(8,128)(2,1)S(1)}, bf16[96,2304]{1,0:T(8,128)(2,1)S(1)}, u32[]{:S(2)}, u32[]{:S(2)}) %collective-permute-start.10) | collective-permute-done | bytes 442400 | tf_op jit(solution)/shard_map/ppermute | solution.py:185
  519.0 6.3 %collective-permute-start.11 = (bf16[192,2304]{1,0:T(8,128)(2,1)S(1)}, bf16[192,2304]{1,0:T(8,128)(2,1)S(1)}, u32[]{:S(2)}, u32[]{:S(2)}) collective-permute-start(bf16[192,2304]{1,0:T(8,128)(2,1)S(1)} %pad_maximum_fusion.6), channel_id=1, source_target_pairs={{0,2},{2,0},{4,6},{6,4},{8,10},{10,8},{12,14},{14,12},{1,3},{3,1},... | collective-permute-start | bytes 2654216 | tf_op jit(solution)/shard_map/ppermute | solution.py:185
  (379 shorter events, 181.1 us)
Async XLA Ops:
  7.3 179.9 %all-gather.4.cloned.1.call-start = ((), (), s32[]{:S(2)}) async-start(), calls=%async_computation.4 | async-start | bytes 1769472 | tf_op jit(solution)/shard_map/all_gather | solution.py:262
  8.0 181.9 %all-gather.6.cloned.1.call-start = ((), (), s32[]{:S(2)}) async-start(), calls=%async_computation.5 | async-start | bytes 7077888 | tf_op jit(solution)/shard_map/all_gather | solution.py:263
  9.3 30.3 %collective-permute-start.1 = (bf16[192,2304]{1,0:T(8,128)(2,1)S(1)}, bf16[192,2304]{1,0:T(8,128)(2,1)S(1)}, u32[]{:S(2)}, u32[]{:S(2)}) collective-permute-start(bf16[192,2304]{1,0:T(8,128)(2,1)S(1)} %dynamic-slice_bitcast_fusion.6), channel_id=1, source_target_pairs={{0,1},{1,0},{2,3},{3,2},{4,5},{5,4},{6,7},{7,6},{8,9},{9,8},{10,11... | collective-permute-start | bytes 2654216 | tf_op jit(solution)/shard_map/ppermute | solution.py:185
  13.2 30.4 %collective-permute-start = (bf16[1,4608]{1,0:T(2,128)(2,1)S(1)}, bf16[1,4608]{1,0:T(2,128)(2,1)S(1)}, u32[]{:S(2)}, u32[]{:S(2)}) collective-permute-start(bf16[1,4608]{1,0:T(2,128)(2,1)S(1)} %reshape.373), channel_id=1, source_target_pairs={{0,1},{1,0},{2,3},{3,2},{4,5},{5,4},{6,7},{7,6},{8,9},{9,8},{10,11... | collective-permute-start | bytes 27656 | tf_op jit(solution)/shard_map/ppermute | solution.py:185
  65.0 59.4 %all-to-all-start = ((bf16[8,256,576]{1,2,0:T(8,128)(2,1)}), bf16[8,256,576]{1,2,0:T(8,128)(2,1)S(1)}, u32[]{:S(2)}, u32[]{:S(2)}) async-start(bf16[8,256,576]{1,2,0:T(8,128)(2,1)} %bitcast.254), calls=%async_computation | async-start | bytes 4718592 | tf_op jit(solution)/shard_map/all_to_all | solution.py:166
  70.6 126.5 %all-gather.8.cloned.1.call-start = ((), (), s32[]{:S(2)}) async-start(), calls=%async_computation.6 | async-start | bytes 7077888 | tf_op jit(solution)/shard_map/all_gather | solution.py:264
  160.5 24.8 %all-to-all-start.1 = ((bf16[8,256,192]{1,2,0:T(8,128)(2,1)}), bf16[8,256,192]{1,2,0:T(8,128)(2,1)S(1)}, u32[]{:S(2)}, u32[]{:S(2)}) async-start(bf16[8,256,192]{1,2,0:T(8,128)(2,1)} %copy.54), calls=%async_computation.1 | async-start | bytes 1572864 | tf_op jit(solution)/shard_map/all_to_all | solution.py:177
  237.9 12.2 %collective-permute-start.14 = (bf16[96,768]{1,0:T(8,128)(2,1)}, bf16[96,768]{1,0:T(8,128)(2,1)}, u32[]{:S(2)}, u32[]{:S(2)}) collective-permute-start(bf16[96,768]{1,0:T(8,128)(2,1)} %dynamic-slice_bitcast_fusion.17), channel_id=1, source_target_pairs={{0,16},{16,0},{1,17},{17,1},{2,18},{18,2},{3,19},{19,3},{4,20},{20... | collective-permute-start | bytes 442376 | tf_op jit(solution)/shard_map/ppermute | solution.py:185
  245.5 37.4 %all-to-all-start.2 = ((bf16[8,256,192]{1,2,0:T(8,128)(2,1)}), bf16[8,256,192]{1,2,0:T(8,128)(2,1)S(1)}, u32[]{:S(2)}, u32[]{:S(2)}) async-start(bf16[8,256,192]{1,2,0:T(8,128)(2,1)} %bitcast.274), calls=%async_computation.2 | async-start | bytes 1572864 | tf_op jit(solution)/shard_map/all_to_all | solution.py:166
  251.1 13.7 %collective-permute-start.15 = (bf16[48,768]{1,0:T(8,128)(2,1)S(1)}, bf16[48,768]{1,0:T(8,128)(2,1)S(1)}, u32[]{:S(2)}, u32[]{:S(2)}) collective-permute-start(bf16[48,768]{1,0:T(8,128)(2,1)S(1)} %dynamic-slice_bitcast_fusion.19), channel_id=1, source_target_pairs={{0,4},{2,6},{4,0},{6,2},{8,12},{10,14},{12,8},{14,10},{1,5},{3,7},... | collective-permute-start | bytes 221192 | tf_op jit(solution)/shard_map/ppermute | solution.py:185
  256.0 55.3 %collective-permute-start.21 = (bf16[2,192,3072]{2,1,0:T(8,128)(2,1)}, bf16[2,192,3072]{2,1,0:T(8,128)(2,1)}, u32[]{:S(2)}, u32[]{:S(2)}) collective-permute-start(bf16[2,192,3072]{2,1,0:T(8,128)(2,1)} %dynamic-slice_bitcast_fusion.1), channel_id=1, source_target_pairs={{0,2},{2,0},{4,6},{6,4},{8,10},{10,8},{12,14},{14,12},{1,3},{3,1},... | collective-permute-start | bytes 7077896 | tf_op jit(solution)/shard_map/ppermute | solution.py:185
  280.8 59.9 %collective-permute-start.30 = (bf16[2,768,768]{2,1,0:T(8,128)(2,1)}, bf16[2,768,768]{2,1,0:T(8,128)(2,1)}, u32[]{:S(2)}, u32[]{:S(2)}) collective-permute-start(bf16[2,768,768]{2,1,0:T(8,128)(2,1)} %dynamic-slice_bitcast_fusion), channel_id=1, source_target_pairs={{0,2},{2,0},{4,6},{6,4},{8,10},{10,8},{12,14},{14,12},{1,3},{3,1},... | collective-permute-start | bytes 7077896 | tf_op jit(solution)/shard_map/ppermute | solution.py:185
  282.7 56.8 %collective-permute-start.19 = (bf16[96,768]{1,0:T(8,128)(2,1)S(1)}, bf16[96,768]{1,0:T(8,128)(2,1)}, u32[]{:S(2)}, u32[]{:S(2)}) collective-permute-start(bf16[96,768]{1,0:T(8,128)(2,1)S(1)} %pad_maximum_fusion.14), channel_id=1, source_target_pairs={{0,16},{16,0},{1,17},{17,1},{2,18},{18,2},{3,19},{19,3},{4,20},{20... | collective-permute-start | bytes 442376 | tf_op jit(solution)/shard_map/ppermute | solution.py:185
  317.3 27.0 %collective-permute-start.22 = (bf16[192,3072]{1,0:T(8,128)(2,1)}, bf16[192,3072]{1,0:T(8,128)(2,1)}, u32[]{:S(2)}, u32[]{:S(2)}) collective-permute-start(bf16[192,3072]{1,0:T(8,128)(2,1)} %dynamic-slice_bitcast_fusion.4), channel_id=1, source_target_pairs={{0,1},{1,0},{2,3},{3,2},{4,5},{5,4},{6,7},{7,6},{8,9},{9,8},{10,11... | collective-permute-start | bytes 3538952 | tf_op jit(solution)/shard_map/ppermute | solution.py:185
  331.9 101.5 %all-to-all-start.3 = ((bf16[8,256,576]{1,2,0:T(8,128)(2,1)}), bf16[8,256,576]{1,2,0:T(8,128)(2,1)}, u32[]{:S(2)}, u32[]{:S(2)}) async-start(bf16[8,256,576]{1,2,0:T(8,128)(2,1)} %copy.61), calls=%async_computation.3 | async-start | bytes 4718592 | tf_op jit(solution)/shard_map/all_to_all | solution.py:177
  343.8 27.4 %collective-permute-start.31 = (bf16[768,768]{1,0:T(8,128)(2,1)S(1)}, bf16[768,768]{1,0:T(8,128)(2,1)S(1)}, u32[]{:S(2)}, u32[]{:S(2)}) collective-permute-start(bf16[768,768]{1,0:T(8,128)(2,1)S(1)} %dynamic-slice_bitcast_fusion.3), channel_id=1, source_target_pairs={{0,1},{1,0},{2,3},{3,2},{4,5},{5,4},{6,7},{7,6},{8,9},{9,8},{10,11... | collective-permute-start | bytes 3538952 | tf_op jit(solution)/shard_map/ppermute | solution.py:185
  347.1 25.8 %collective-permute-start.23 = (bf16[96,3072]{1,0:T(8,128)(2,1)S(1)}, bf16[96,3072]{1,0:T(8,128)(2,1)S(1)}, u32[]{:S(2)}, u32[]{:S(2)}) collective-permute-start(bf16[96,3072]{1,0:T(8,128)(2,1)S(1)} %dynamic-slice_bitcast_fusion.8), channel_id=1, source_target_pairs={{0,16},{16,0},{1,17},{17,1},{2,18},{18,2},{3,19},{19,3},{4,20},{20... | collective-permute-start | bytes 1769480 | tf_op jit(solution)/shard_map/ppermute | solution.py:185
  371.5 13.8 %collective-permute-start.32 = (bf16[384,768]{1,0:T(8,128)(2,1)S(1)}, bf16[384,768]{1,0:T(8,128)(2,1)S(1)}, u32[]{:S(2)}, u32[]{:S(2)}) collective-permute-start(bf16[384,768]{1,0:T(8,128)(2,1)S(1)} %dynamic-slice_bitcast_fusion.7), channel_id=1, source_target_pairs={{0,16},{16,0},{1,17},{17,1},{2,18},{18,2},{3,19},{19,3},{4,20},{20... | collective-permute-start | bytes 1769480 | tf_op jit(solution)/shard_map/ppermute | solution.py:185
  373.1 14.6 %collective-permute-start.24 = (bf16[48,3072]{1,0:T(8,128)(2,1)S(1)}, bf16[48,3072]{1,0:T(8,128)(2,1)S(1)}, u32[]{:S(2)}, u32[]{:S(2)}) collective-permute-start(bf16[48,3072]{1,0:T(8,128)(2,1)S(1)} %dynamic-slice_bitcast_fusion.12), channel_id=1, source_target_pairs={{0,4},{2,6},{4,0},{6,2},{8,12},{10,14},{12,8},{14,10},{1,5},{3,7},... | collective-permute-start | bytes 884744 | tf_op jit(solution)/shard_map/ppermute | solution.py:185
  385.5 17.5 %collective-permute-start.33 = (bf16[192,768]{1,0:T(8,128)(2,1)S(1)}, bf16[192,768]{1,0:T(8,128)(2,1)S(1)}, u32[]{:S(2)}, u32[]{:S(2)}) collective-permute-start(bf16[192,768]{1,0:T(8,128)(2,1)S(1)} %dynamic-slice_bitcast_fusion.11), channel_id=1, source_target_pairs={{0,4},{2,6},{4,0},{6,2},{8,12},{10,14},{12,8},{14,10},{1,5},{3,7},... | collective-permute-start | bytes 884744 | tf_op jit(solution)/shard_map/ppermute | solution.py:185
  387.8 15.5 %collective-permute-start.25 = (bf16[24,3072]{1,0:T(8,128)(2,1)S(1)}, bf16[24,3072]{1,0:T(8,128)(2,1)S(1)}, u32[]{:S(2)}, u32[]{:S(2)}) collective-permute-start(bf16[24,3072]{1,0:T(8,128)(2,1)S(1)} %dynamic-slice_bitcast_fusion.16), channel_id=1, source_target_pairs={{0,8},{2,10},{4,12},{6,14},{8,0},{10,2},{12,4},{14,6},{1,9},{3,11}... | collective-permute-start | bytes 442376 | tf_op jit(solution)/shard_map/ppermute | solution.py:185
  403.2 12.0 %collective-permute-start.34 = (bf16[96,768]{1,0:T(8,128)(2,1)S(1)}, bf16[96,768]{1,0:T(8,128)(2,1)S(1)}, u32[]{:S(2)}, u32[]{:S(2)}) collective-permute-start(bf16[96,768]{1,0:T(8,128)(2,1)S(1)} %dynamic-slice_bitcast_fusion.15), channel_id=1, source_target_pairs={{0,8},{2,10},{4,12},{6,14},{8,0},{10,2},{12,4},{14,6},{1,9},{3,11}... | collective-permute-start | bytes 442376 | tf_op jit(solution)/shard_map/ppermute | solution.py:185
  403.3 15.1 %collective-permute-start.26 = (bf16[24,3072]{1,0:T(8,128)(2,1)S(1)}, bf16[24,3072]{1,0:T(8,128)(2,1)S(1)}, u32[]{:S(2)}, u32[]{:S(2)}) collective-permute-start(bf16[24,3072]{1,0:T(8,128)(2,1)S(1)} %fusion.39), channel_id=1, source_target_pairs={{0,8},{2,10},{4,12},{6,14},{8,0},{10,2},{12,4},{14,6},{1,9},{3,11}... | collective-permute-start | bytes 442376 | tf_op jit(solution)/shard_map/ppermute | solution.py:185
  418.4 12.6 %collective-permute-start.27 = (bf16[48,3072]{1,0:T(8,128)(2,1)S(1)}, bf16[48,3072]{1,0:T(8,128)(2,1)S(1)}, u32[]{:S(2)}, u32[]{:S(2)}) collective-permute-start(bf16[48,3072]{1,0:T(8,128)(2,1)S(1)} %pad_maximum_fusion.11), channel_id=1, source_target_pairs={{0,4},{2,6},{4,0},{6,2},{8,12},{10,14},{12,8},{14,10},{1,5},{3,7},... | collective-permute-start | bytes 884744 | tf_op jit(solution)/shard_map/ppermute | solution.py:185
  425.6 30.6 %collective-permute-start.36 = (bf16[192,768]{1,0:T(8,128)(2,1)}, bf16[192,768]{1,0:T(8,128)(2,1)}, u32[]{:S(2)}, u32[]{:S(2)}) collective-permute-start(bf16[192,768]{1,0:T(8,128)(2,1)} %pad_maximum_fusion.12), channel_id=1, source_target_pairs={{0,4},{2,6},{4,0},{6,2},{8,12},{10,14},{12,8},{14,10},{1,5},{3,7},... | collective-permute-start | bytes 884744 | tf_op jit(solution)/shard_map/ppermute | solution.py:185
  432.1 61.4 %collective-permute-start.28 = (bf16[96,3072]{1,0:T(8,128)(2,1)}, bf16[96,3072]{1,0:T(8,128)(2,1)}, u32[]{:S(2)}, u32[]{:S(2)}) collective-permute-start(bf16[96,3072]{1,0:T(8,128)(2,1)} %pad_maximum_fusion.7), channel_id=1, source_target_pairs={{0,16},{16,0},{1,17},{17,1},{2,18},{18,2},{3,19},{19,3},{4,20},{20... | collective-permute-start | bytes 1769480 | tf_op jit(solution)/shard_map/ppermute | solution.py:185
  454.9 20.9 %collective-permute-start.4 = (bf16[192,2304]{1,0:T(8,128)(2,1)S(1)}, bf16[192,2304]{1,0:T(8,128)(2,1)S(1)}, u32[]{:S(2)}, u32[]{:S(2)}) collective-permute-start(bf16[192,2304]{1,0:T(8,128)(2,1)S(1)} %dynamic-slice_bitcast_fusion.5), channel_id=1, source_target_pairs={{0,1},{1,0},{2,3},{3,2},{4,5},{5,4},{6,7},{7,6},{8,9},{9,8},{10,11... | collective-permute-start | bytes 2654216 | tf_op jit(solution)/shard_map/ppermute | solution.py:185
  457.5 50.0 %collective-permute-start.37 = (bf16[384,768]{1,0:T(8,128)(2,1)S(1)}, bf16[384,768]{1,0:T(8,128)(2,1)S(1)}, u32[]{:S(2)}, u32[]{:S(2)}) collective-permute-start(bf16[384,768]{1,0:T(8,128)(2,1)S(1)} %pad_maximum_fusion.8), channel_id=1, source_target_pairs={{0,16},{16,0},{1,17},{17,1},{2,18},{18,2},{3,19},{19,3},{4,20},{20... | collective-permute-start | bytes 1769480 | tf_op jit(solution)/shard_map/ppermute | solution.py:185
  460.3 16.1 %collective-permute-start.42 = (f32[1,4608]{1,0:T(1,128)S(1)}, f32[1,4608]{1,0:T(1,128)S(1)}, u32[]{:S(2)}, u32[]{:S(2)}) collective-permute-start(f32[1,4608]{1,0:T(1,128)S(1)} %add.373), channel_id=1, source_target_pairs={{0,8},{2,10},{4,12},{6,14},{8,0},{10,2},{12,4},{14,6},{1,9},{3,11}... | collective-permute-start | bytes 55304 | tf_op jit(solution)/shard_map/ppermute | solution.py:185
  498.3 13.6 %collective-permute-start.29 = (bf16[192,3072]{1,0:T(8,128)(2,1)S(1)}, bf16[192,3072]{1,0:T(8,128)(2,1)S(1)}, u32[]{:S(2)}, u32[]{:S(2)}) collective-permute-start(bf16[192,3072]{1,0:T(8,128)(2,1)S(1)} %pad_maximum_fusion.4), channel_id=1, source_target_pairs={{0,2},{2,0},{4,6},{6,4},{8,10},{10,8},{12,14},{14,12},{1,3},{3,1},... | collective-permute-start | bytes 3538952 | tf_op jit(solution)/shard_map/ppermute | solution.py:185
  507.8 17.6 %collective-permute-start.38 = (bf16[768,768]{1,0:T(8,128)(2,1)S(1)}, bf16[768,768]{1,0:T(8,128)(2,1)S(1)}, u32[]{:S(2)}, u32[]{:S(2)}) collective-permute-start(bf16[768,768]{1,0:T(8,128)(2,1)S(1)} %pad_maximum_fusion.5), channel_id=1, source_target_pairs={{0,2},{2,0},{4,6},{6,4},{8,10},{10,8},{12,14},{14,12},{1,3},{3,1},... | collective-permute-start | bytes 3538952 | tf_op jit(solution)/shard_map/ppermute | solution.py:185
  519.0 12.1 %collective-permute-start.11 = (bf16[192,2304]{1,0:T(8,128)(2,1)S(1)}, bf16[192,2304]{1,0:T(8,128)(2,1)S(1)}, u32[]{:S(2)}, u32[]{:S(2)}) collective-permute-start(bf16[192,2304]{1,0:T(8,128)(2,1)S(1)} %pad_maximum_fusion.6), channel_id=1, source_target_pairs={{0,2},{2,0},{4,6},{6,4},{8,10},{10,8},{12,14},{14,12},{1,3},{3,1},... | collective-permute-start | bytes 2654216 | tf_op jit(solution)/shard_map/ppermute | solution.py:185
  (72 other events, 494.4 us)
Sparse Core Ops, SparseCore 0:
  9.7 35.1 all-gather.3
  46.4 63.9 all-gather.5
  111.9 62.6 all-gather.7
